TPU v7x, 32 devices: a whole 2x2x4 slice. The times are simulated.
32 devices in a mesh: dp: 4 (over y, core), frame: 2 (over x), tensor: 4 (over z).
Axes of the slice: x: 2, y: 2, z: 4, core: 2. Of those that a mesh axis runs over, the one named last changes fastest.
Arguments:
- latent: bfloat16 [12, 16, 32, 128], P('dp', 'frame', 'tensor'), may hold values from -5 to 5
- noise_draw: bfloat16 [12, 16, 32, 128], P('dp', 'frame', 'tensor'), may hold values from -5 to 5
- levels: int32 [12, 16], P('dp', 'frame'), may hold values from 1 to 999
- context: int32 [12], replicated, may hold values from 1 to 15
- step_count: int32 [1], replicated, may hold values from 1 to 20
- w_in: float32 [1024, 7168], P(('dp', 'frame'), 'tensor'), may hold values from -0.1875 to 0.1875
- w_outs: float32 [5120, 1024], P('tensor', ('dp', 'frame')), may hold values from -2 to 2, as said below
- w_cond: float32 [1024, 8192], P(('dp', 'frame'), 'tensor'), may hold values from -0.1875 to 0.1875
- w_time: float32 [1280, 1024], P(('dp', 'frame')), may hold values from -0.5 to 0.5
- w_patch: float32 [2, 16, 1024], P(None, None, ('dp', 'frame')), may hold values from -0.75 to 0.75
- m_in: float32 [1024, 7168], P(('dp', 'frame'), 'tensor'), may hold values from -0.00012207031 to 0.00012207031
- m_outs: float32 [5120, 1024], P('tensor', ('dp', 'frame')), may hold values from -3.8146973e-05 to 3.8146973e-05
- m_cond: float32 [1024, 8192], P(('dp', 'frame'), 'tensor'), may hold values from -0.00012207031 to 0.00012207031
- m_time: float32 [1280, 1024], P(('dp', 'frame')), may hold values from -0.00012207031 to 0.00012207031
- m_patch: float32 [2, 16, 1024], P(None, None, ('dp', 'frame')), may hold values from -0.00012207031 to 0.00012207031
- v_in: float32 [1024, 7168], P(('dp', 'frame'), 'tensor'), may hold values from 4.481289e-10 to 1.7925156e-09
- v_outs: float32 [5120, 1024], P('tensor', ('dp', 'frame')), may hold values from 4.481289e-11 to 1.7925156e-10
- v_cond: float32 [1024, 8192], P(('dp', 'frame'), 'tensor'), may hold values from 4.481289e-10 to 1.7925156e-09
- v_time: float32 [1280, 1024], P(('dp', 'frame')), may hold values from 4.481289e-10 to 1.7925156e-09
- v_patch: float32 [2, 16, 1024], P(None, None, ('dp', 'frame')), may hold values from 4.481289e-10 to 1.7925156e-09
Outputs:
- loss_value: float32 [], replicated
- grad_norm: float32 [], replicated
- new_in: float32 [1024, 7168], P(('dp', 'frame'), 'tensor')
- new_outs: float32 [5120, 1024], P('tensor', ('dp', 'frame'))
- new_cond: float32 [1024, 8192], P(('dp', 'frame'), 'tensor')
- new_time: float32 [1280, 1024], P(('dp', 'frame'))
- new_patch: float32 [2, 16, 1024], P(None, None, ('dp', 'frame'))
- first_in: float32 [1024, 7168], P(('dp', 'frame'), 'tensor')
- first_outs: float32 [5120, 1024], P('tensor', ('dp', 'frame'))
- first_cond: float32 [1024, 8192], P(('dp', 'frame'), 'tensor')
- first_time: float32 [1280, 1024], P(('dp', 'frame'))
- first_patch: float32 [2, 16, 1024], P(None, None, ('dp', 'frame'))
- second_in: float32 [1024, 7168], P(('dp', 'frame'), 'tensor')
- second_outs: float32 [5120, 1024], P('tensor', ('dp', 'frame'))
- second_cond: float32 [1024, 8192], P(('dp', 'frame'), 'tensor')
- second_time: float32 [1280, 1024], P(('dp', 'frame'))
- second_patch: float32 [2, 16, 1024], P(None, None, ('dp', 'frame'))
- half_in: bfloat16 [1024, 7168], P(('dp', 'frame'), 'tensor')
- half_outs: bfloat16 [5120, 1024], P('tensor', ('dp', 'frame'))
- half_cond: bfloat16 [1024, 8192], P(('dp', 'frame'), 'tensor')
- half_time: bfloat16 [1280, 1024], P(('dp', 'frame'))
- half_patch: bfloat16 [2, 16, 1024], P(None, None, ('dp', 'frame'))
Inputs may be any that keep to these rules, and one draw needn't show every extreme that they name: `w_outs`: output-projection and down-projection weights.
All inputs are finite; a program needn't handle non-finite values.
Results may differ from a plain program's by a relative error of at most 0.017.
Values may be sent and summed in bfloat16 or wider, within the bound.
A program may use at most 512 MiB of HBM per device.

v0:
```python
from functools import partial
import math

import jax
import jax.numpy as jnp
from jax import lax
from jax.experimental import pallas as pl
from jax.experimental.pallas import tpu as pltpu
from jax.sharding import PartitionSpec as P

D = 1024
HD = 64
TEMB = 256
CHANNELS = 4
PATCH = 2
PD = 16
TOKF = 256
FRAMES = 16
NLEV = 1000
PAIR = 2 * HD
PLANE = ("dp", "frame")
EVERY = ("tensor", "dp", "frame")
SCORE_SCALE = HD ** (-0.5) * math.log2(math.e)
TOTAL_LOW = 2.0**-40
TOTAL_HIGH = 2.0**70


EPS_NORM = 1e-06
MAX_NORM = 0.1
LEARN_RATE = 0.08
WEIGHT_DECAY = 0.1
BETA_FIRST = 0.5
BETA_SECOND = 0.5
ADAM_EPS = 1e-08


def to_half(array_in):
    return array_in.astype(jnp.bfloat16)


def product(left_mat, right_mat):
    return jnp.dot(left_mat, right_mat, preferred_element_type=jnp.float32)


def rows_product(left_mat, right_mat):
    return lax.dot_general(
        left_mat, right_mat, (((0,), (0,)), ((), ())), preferred_element_type=jnp.float32
    )


def cols_product(left_mat, right_mat):
    return lax.dot_general(
        left_mat, right_mat, (((1,), (1,)), ((), ())), preferred_element_type=jnp.float32
    )


def frequency_table(level_values):
    half_width = TEMB // 2
    rate_table = jnp.exp(
        -math.log(10000.0) * jnp.arange(half_width, dtype=jnp.float32) / half_width
    )
    angles = level_values[..., None] * rate_table
    return jnp.concatenate([jnp.cos(angles), jnp.sin(angles)], axis=-1)


def noise_terms(level_values):
    angles = level_values * (0.5 * math.pi / NLEV)
    return (jnp.cos(angles), jnp.sin(angles))


def patchify(field_in):
    lead_shape = field_in.shape[:-2]
    rows_here = field_in.shape[-2]
    width_cells = field_in.shape[-1] // CHANNELS
    lead_rank = len(lead_shape)
    blocks_view = field_in.reshape(
        lead_shape + (rows_here // PATCH, PATCH, width_cells // PATCH, PATCH, CHANNELS)
    )
    order_axes = tuple(range(lead_rank)) + (
        lead_rank,
        lead_rank + 2,
        lead_rank + 1,
        lead_rank + 3,
        lead_rank + 4,
    )
    return jnp.transpose(blocks_view, order_axes).reshape(
        lead_shape + (rows_here // PATCH * (width_cells // PATCH), PATCH * PATCH * CHANNELS)
    )


def contract(left_mat, right_mat, left_dim, right_dim):
    return lax.dot_general(
        left_mat,
        right_mat,
        (((left_dim,), (right_dim,)), ((), ())),
        preferred_element_type=jnp.float32,
    )


def head_lanes(head):
    return lax.broadcasted_iota(jnp.int32, (1, PAIR), 1) // HD == head


def attend_kernel(chunk, query_ref, key_ref, value_ref, exps_ref, low_ref, mixed_ref, inverse_ref):
    key_total = key_ref.shape[1]
    block_rows = query_ref.shape[1]
    query_pair = query_ref[0]
    mixed_parts = []
    inverse_parts = []
    for head in range(2):
        lanes = head_lanes(head)
        query_head = jnp.where(lanes, query_pair, jnp.zeros_like(query_pair))

        def scores_of(rows):
            return contract(key_ref[0, rows, :], query_head, 1, 1) * SCORE_SCALE

        def add_chunk(rows, scores, total):
            exps = jnp.exp2(scores).astype(jnp.bfloat16)
            exps_ref[0, head, :, rows] = exps.T
            values = value_ref[0, rows, :]
            values = jnp.where(lanes, values, jnp.ones_like(values))
            return total + contract(values, exps, 0, 0)

        zeros = jnp.zeros((PAIR, block_rows), jnp.float32)
        total = zeros
        for start in range(0, key_total, chunk):
            rows = slice(start, start + chunk)
            total = add_chunk(rows, scores_of(rows), total)
        sum_rows = total[(1 - head) * HD : (1 - head) * HD + 8]
        outside = jnp.max(
            jnp.where((sum_rows > TOTAL_LOW) & (sum_rows < TOTAL_HIGH), 0.0, 1.0)
        )

        def shifted(unused):
            def chunk_rows(step):
                return pl.ds(pl.multiple_of(step * chunk, chunk), chunk)

            def highest(step, top):
                return jnp.maximum(
                    top, jnp.max(scores_of(chunk_rows(step)), axis=0, keepdims=True)
                )

            top = lax.fori_loop(
                0, key_total // chunk, highest, jnp.full((1, block_rows), -jnp.inf, jnp.float32)
            )

            def one_chunk(step, total):
                rows = chunk_rows(step)
                return add_chunk(rows, scores_of(rows) - top, total)

            return lax.fori_loop(0, key_total // chunk, one_chunk, zeros)

        total = lax.cond(outside > 0.0, shifted, lambda kept: kept, total)
        inverse = 1.0 / total[(1 - head) * HD : (2 - head) * HD]
        mixed_parts.append(total[head * HD : (head + 1) * HD] * inverse)
        inverse_parts.append(inverse)
    mixed = jnp.concatenate(mixed_parts, axis=0).T
    mixed_ref[0] = mixed
    low_ref[0] = mixed.astype(jnp.bfloat16)
    inverse_ref[0] = jnp.concatenate(inverse_parts, axis=0).T


def attend(query_in, key_value, key_place):
    units, query_total = query_in.shape[:2]
    key_total = key_value.shape[1]
    block_rows = min(1024, query_total)
    chunk = min(1024, key_total)

    def query_map(unit, step):
        return (unit, step, 0)

    query_spec = pl.BlockSpec((1, block_rows, PAIR), query_map)
    shape_rows = (units, query_total, PAIR)
    products = 4 * units * query_total * key_total * PAIR
    return pl.pallas_call(
        partial(attend_kernel, chunk),
        grid=(units, query_total // block_rows),
        in_specs=[
            query_spec,
            pl.BlockSpec((1, key_total, PAIR), lambda unit, step: (unit, 0, key_place)),
            pl.BlockSpec((1, key_total, PAIR), lambda unit, step: (unit, 0, key_place + 1)),
        ],
        out_specs=[
            pl.BlockSpec((1, 2, block_rows, key_total), lambda unit, step: (unit, 0, step, 0)),
            query_spec,
            query_spec,
            query_spec,
        ],
        out_shape=[
            jax.ShapeDtypeStruct((units, 2, query_total, key_total), jnp.bfloat16),
            jax.ShapeDtypeStruct(shape_rows, jnp.bfloat16),
            jax.ShapeDtypeStruct(shape_rows, jnp.float32),
            jax.ShapeDtypeStruct(shape_rows, jnp.float32),
        ],
        cost_estimate=pl.CostEstimate(
            flops=4 * products,
            bytes_accessed=4 * units * query_total * key_total,
            transcendentals=2 * units * query_total * key_total,
        ),
        compiler_params=pltpu.CompilerParams(vmem_limit_bytes=62 << 20),
    )(query_in, key_value, key_value)


def attend_back_kernel(
    chunk,
    exps_ref,
    query_ref,
    key_ref,
    value_ref,
    grad_ref,
    mixed_ref,
    inverse_ref,
    *grads_and_sums,
):
    *grad_refs, key_sums, value_sums = grads_and_sums
    step = pl.program_id(1)
    head = pl.program_id(2)
    key_total = key_ref.shape[1]
    block_rows = query_ref.shape[1]
    lane = lax.broadcasted_iota(jnp.int32, (1, PAIR), 1)
    lanes = head_lanes(head)
    grad_low = jnp.where(lanes, grad_ref[0].astype(jnp.float32) * inverse_ref[0], 0.0).astype(
        jnp.bfloat16
    )
    row_terms = jnp.sum(grad_low.astype(jnp.float32) * mixed_ref[0], axis=1, keepdims=True)
    term_high = row_terms.astype(jnp.bfloat16).astype(jnp.float32)
    term_rest = row_terms - term_high
    term_lanes = jnp.where(lane == 0, -term_high, jnp.where(lane == 1, -term_rest, 0.0))
    grad_wide = jnp.concatenate([grad_low, term_lanes.astype(jnp.bfloat16)], axis=1)
    query_pair = query_ref[0]
    query_columns = jnp.where(lanes, query_pair, jnp.zeros_like(query_pair)).T
    grad_columns = grad_low.T
    term_ones = jnp.broadcast_to(jnp.where(lane < 2, 1.0, 0.0).astype(jnp.bfloat16), (chunk, PAIR))

    @pl.when((step == 0) & (head == 0))
    def start_sums():
        key_sums[...] = jnp.zeros_like(key_sums)
        value_sums[...] = jnp.zeros_like(value_sums)

    grad_query = jnp.zeros((block_rows, PAIR), jnp.float32)
    for start in range(0, key_total, chunk):
        rows = slice(start, start + chunk)
        values_wide = jnp.concatenate([value_ref[0, rows, :], term_ones], axis=1)
        grad_probs = contract(grad_wide, values_wide, 1, 1).astype(jnp.bfloat16)
        exps = exps_ref[0, 0, :, rows]
        grad_scores = exps * grad_probs
        value_sums[:, rows] += contract(grad_columns, exps, 1, 0)
        key_sums[:, rows] += contract(query_columns, grad_scores, 1, 0)
        keys = key_ref[0, rows, :]
        keys = jnp.where(lanes, keys, jnp.zeros_like(keys))
        grad_query = grad_query + contract(grad_scores, keys, 1, 0)
    grad_query_low = (grad_query * HD ** (-0.5)).astype(jnp.bfloat16)

    fused = len(grad_refs) == 1
    first_row = pl.multiple_of(step * block_rows, block_rows) if fused else 0
    query_place = (0, pl.ds(first_row, block_rows), slice(0, PAIR))

    @pl.when(head == 0)
    def first_head():
        grad_refs[0][query_place] = grad_query_low

    @pl.when(head == 1)
    def second_head():
        grad_refs[0][query_place] = jnp.where(lanes, grad_query_low, grad_refs[0][query_place])

    @pl.when((step == pl.num_programs(1) - 1) & (head == 1))
    def write_sums():
        grad_key = (key_sums[...].T * HD ** (-0.5)).astype(jnp.bfloat16)
        grad_value = value_sums[...].T.astype(jnp.bfloat16)
        if fused:
            grad_refs[0][0, :, PAIR : 2 * PAIR] = grad_key
            grad_refs[0][0, :, 2 * PAIR :] = grad_value
        else:
            grad_refs[1][0] = grad_key
            grad_refs[2][0] = grad_value


def attend_back(exps, query_in, key_value, key_place, grad_mixed, mixed, inverse):
    units, query_total = mixed.shape[:2]
    key_total = key_value.shape[1]
    block_rows = min(1024, query_total)
    chunk = min(1024, key_total)
    query_spec = pl.BlockSpec((1, block_rows, PAIR), lambda unit, step, head: (unit, step, 0))
    whole_spec = pl.BlockSpec((1, key_total, PAIR), lambda unit, step, head: (unit, 0, 0))
    if query_total == key_total:
        out_sizes = [(key_total, 3 * PAIR)]
        out_specs = [
            pl.BlockSpec((1, key_total, 3 * PAIR), lambda unit, step, head: (unit, 0, 0))
        ]
    else:
        out_sizes = [(query_total, PAIR), (key_total, PAIR), (key_total, PAIR)]
        out_specs = [query_spec, whole_spec, whole_spec]
    products = 8 * units * query_total * key_total * PAIR
    return pl.pallas_call(
        partial(attend_back_kernel, chunk),
        grid=(units, query_total // block_rows, 2),
        in_specs=[
            pl.BlockSpec(
                (1, 1, block_rows, key_total), lambda unit, step, head: (unit, head, step, 0)
            ),
            query_spec,
            pl.BlockSpec((1, key_total, PAIR), lambda unit, step, head: (unit, 0, key_place)),
            pl.BlockSpec((1, key_total, PAIR), lambda unit, step, head: (unit, 0, key_place + 1)),
            query_spec,
            query_spec,
            query_spec,
        ],
        out_specs=out_specs,
        out_shape=[
            jax.ShapeDtypeStruct((units, rows, columns), jnp.bfloat16)
            for rows, columns in out_sizes
        ],
        scratch_shapes=[pltpu.VMEM((PAIR, key_total), jnp.float32)] * 2,
        cost_estimate=pl.CostEstimate(
            flops=4 * products,
            bytes_accessed=4 * units * query_total * key_total,
            transcendentals=0,
        ),
        compiler_params=pltpu.CompilerParams(vmem_limit_bytes=62 << 20),
    )(exps, query_in, key_value, key_value, grad_mixed, mixed, inverse)


def normalize(rows_in):
    centre = rows_in - jnp.mean(rows_in, axis=-1, keepdims=True)
    spread = jnp.mean(centre * centre, axis=-1, keepdims=True)
    inverse = lax.rsqrt(spread + EPS_NORM)
    return (centre * inverse, inverse)


def normalize_back(normed, inverse, scale_row, grad_out):
    grad_shift = jnp.sum(grad_out, axis=0, keepdims=True)
    grad_scale = jnp.sum(grad_out * normed, axis=0, keepdims=True)
    grad_normed = grad_out * (1.0 + scale_row)
    grad_rows = inverse * (
        grad_normed
        - jnp.mean(grad_normed, axis=-1, keepdims=True)
        - normed * jnp.mean(grad_normed * normed, axis=-1, keepdims=True)
    )
    return (grad_rows, grad_shift, grad_scale)


def mod_row(mods_ref, place, group):
    return mods_ref[pl.ds(group, 1), place * D : (place + 1) * D]


def group_rows(group, rows_group):
    return pl.ds(pl.multiple_of(group * rows_group, rows_group), rows_group)


def open_kernel(patch_ref, embed_ref, mods_ref, weight_ref, rows_ref, normed_ref, send_ref):
    groups = mods_ref.shape[0]
    rows_group = rows_ref.shape[0] // groups

    @pl.when(pl.program_id(0) == 0)
    def embed_rows():
        def one_group(group, unused):
            rows = group_rows(group, rows_group)
            residual = product(patch_ref[rows, :], embed_ref[...])
            rows_ref[rows, :] = residual
            normed, unused_inverse = normalize(residual)
            normed_ref[rows, :] = to_half(
                normed * (1.0 + mod_row(mods_ref, 1, group)) + mod_row(mods_ref, 0, group)
            )
            return unused

        lax.fori_loop(0, groups, one_group, 0)

    columns = send_ref.shape[2]
    for place in range(send_ref.shape[0]):
        send_ref[place] = to_half(
            product(
                normed_ref[...], weight_ref[0, :, place * columns : (place + 1) * columns]
            )
        )


def open_layer(patch_rows, w_embed, mods, w_qkv):
    tokens = patch_rows.shape[0]
    blocks, unused, columns = w_qkv.shape
    per_block = columns // (3 * PAIR)
    whole = pl.BlockSpec((tokens, D), lambda step: (0, 0))
    return pl.pallas_call(
        open_kernel,
        grid=(blocks,),
        in_specs=[
            pl.BlockSpec(patch_rows.shape, lambda step: (0, 0)),
            pl.BlockSpec(w_embed.shape, lambda step: (0, 0)),
            pl.BlockSpec(mods.shape, lambda step: (0, 0)),
            pl.BlockSpec((1, D, columns), lambda step: (step, 0, 0)),
        ],
        out_specs=[
            whole,
            whole,
            pl.BlockSpec((per_block, tokens, 3 * PAIR), lambda step: (step, 0, 0)),
        ],
        out_shape=[
            jax.ShapeDtypeStruct((tokens, D), jnp.float32),
            jax.ShapeDtypeStruct((tokens, D), jnp.bfloat16),
            jax.ShapeDtypeStruct((blocks * per_block, tokens, 3 * PAIR), jnp.bfloat16),
        ],
        cost_estimate=pl.CostEstimate(
            flops=2 * tokens * D * blocks * columns,
            bytes_accessed=2 * blocks * D * columns + 12 * tokens * D,
            transcendentals=0,
        ),
        compiler_params=pltpu.CompilerParams(vmem_limit_bytes=60 << 20),
    )(patch_rows, w_embed, mods, w_qkv)


GELU_RATE = math.sqrt(2.0 / math.pi)
GELU_CUBE = 0.044715


def middle_kernel(
    head_cols,
    hidden_cols,
    mixed_ref,
    rows_ref,
    mods_ref,
    goal_ref,
    coef_ref,
    head_ref,
    weights_hbm,
    normed_hbm,
    act_hbm,
    grad_mlp_hbm,
    grad_hidden_hbm,
    grad_attn_hbm,
    grad_rows_hbm,
    send_ref,
    grad_mods_ref,
    grad_head_ref,
    loss_ref,
    weights,
    normed_low,
    act_low,
    grad_mlp_low,
    grad_hidden_low,
    grad_attn_low,
    grad_rows,
    attn_sum,
    middle,
    mlp_sum,
    slopes,
    out_sems,
    wide_sems,
    act_sems,
    hidden_sems,
    row_sems,
):
    blocks = weights.shape[0]
    groups = mods_ref.shape[0]
    rows_group = rows_ref.shape[0] // groups
    per_block = head_cols // PAIR
    wide = 2 * hidden_cols
    up_columns = slice(0, hidden_cols)
    down_columns = slice(hidden_cols, wide)
    out_columns = slice(wide, wide + head_cols)

    def fetch_out(block):
        return pltpu.make_async_copy(
            weights_hbm.at[block, :, out_columns],
            weights.at[block, :, out_columns],
            out_sems.at[block],
        )

    def fetch_wide(block):
        return pltpu.make_async_copy(
            weights_hbm.at[block, :, 0:wide], weights.at[block, :, 0:wide], wide_sems.at[block]
        )

    def put_act(block):
        columns = pl.ds(pl.multiple_of(block * hidden_cols, hidden_cols), hidden_cols)
        return pltpu.make_async_copy(
            act_low.at[block], act_hbm.at[:, columns], act_sems.at[block]
        )

    def put_hidden(block):
        columns = pl.ds(pl.multiple_of(block * hidden_cols, hidden_cols), hidden_cols)
        return pltpu.make_async_copy(
            grad_hidden_low.at[block], grad_hidden_hbm.at[:, columns], hidden_sems.at[block]
        )

    put_normed = pltpu.make_async_copy(normed_low, normed_hbm, row_sems.at[0])
    put_grad_mlp = pltpu.make_async_copy(grad_mlp_low, grad_mlp_hbm, row_sems.at[1])
    put_grad_attn = pltpu.make_async_copy(grad_attn_low, grad_attn_hbm, row_sems.at[2])
    put_grad_rows = pltpu.make_async_copy(grad_rows, grad_rows_hbm, row_sems.at[3])

    def each_block(one_block):
        def step(block, unused):
            one_block(block)
            return unused

        lax.fori_loop(0, blocks, step, 0)

    def each_group(one_group):
        def step(group, unused):
            one_group(group, group_rows(group, rows_group))
            return unused

        lax.fori_loop(0, groups, step, 0)

    each_block(lambda block: fetch_out(block).start())
    each_block(lambda block: fetch_wide(block).start())
    attn_sum[...] = jnp.zeros_like(attn_sum)
    mlp_sum[...] = jnp.zeros_like(mlp_sum)

    def attn_out(block):
        fetch_out(block).wait()
        mixed = jnp.concatenate(
            [mixed_ref[block * per_block + place] for place in range(per_block)], axis=1
        )
        attn_sum[...] += contract(mixed, weights[block, :, out_columns], 1, 1)

    each_block(attn_out)

    def to_middle(group, rows):
        residual = rows_ref[rows, :] + mod_row(mods_ref, 2, group) * attn_sum[rows, :]
        middle[rows, :] = residual
        normed, unused_inverse = normalize(residual)
        normed_low[rows, :] = to_half(
            normed * (1.0 + mod_row(mods_ref, 4, group)) + mod_row(mods_ref, 3, group)
        )

    each_group(to_middle)
    put_normed.start()

    def forward_mlp(block):
        fetch_wide(block).wait()
        hidden = product(normed_low[...], weights[block, :, up_columns])
        square = hidden * hidden
        bend = jnp.tanh(GELU_RATE * hidden * (1.0 + GELU_CUBE * square))
        half_open = 0.5 * (1.0 + bend)
        act = to_half(hidden * half_open)
        act_low[block] = act
        slope = half_open + 0.5 * hidden * (1.0 - bend * bend) * (
            GELU_RATE * (1.0 + 3.0 * GELU_CUBE * square)
        )
        slopes[block] = to_half(slope)
        put_act(block).start()
        mlp_sum[...] += contract(act, weights[block, :, down_columns], 1, 1)

    each_block(forward_mlp)
    grad_head_ref[...] = jnp.zeros_like(grad_head_ref)
    loss_ref[...] = jnp.zeros_like(loss_ref)

    def turn(group, rows):
        mlp_out = mlp_sum[rows, :]
        gate = mod_row(mods_ref, 5, group)
        normed, inverse = normalize(middle[rows, :] + gate * mlp_out)
        scale_row = mod_row(mods_ref, 7, group)
        final_low = to_half(normed * (1.0 + scale_row) + mod_row(mods_ref, 6, group))
        error_rows = contract(final_low, head_ref[...], 1, 1) - goal_ref[rows, :]
        weighted = coef_ref[pl.ds(group, 1), :] * error_rows
        loss_ref[pl.ds(0, 1), :] += jnp.sum(weighted * error_rows, axis=0, keepdims=True)
        grad_pred = to_half(2.0 * weighted)
        grad_head_ref[...] += contract(grad_pred, final_low, 0, 0)
        grad_final = product(grad_pred, head_ref[...])
        grad_residual, grad_six, grad_seven = normalize_back(
            normed, inverse, scale_row, grad_final
        )
        grad_mods_ref[4, pl.ds(group, 1), :] = grad_six
        grad_mods_ref[5, pl.ds(group, 1), :] = grad_seven
        grad_mods_ref[3, pl.ds(group, 1), :] = jnp.sum(
            mlp_out * grad_residual, axis=0, keepdims=True
        )
        grad_rows[rows, :] = grad_residual
        grad_mlp_low[rows, :] = to_half(gate * grad_residual)

    each_group(turn)
    put_grad_mlp.start()
    mlp_sum[...] = jnp.zeros_like(mlp_sum)

    def backward_mlp(block):
        grad_act = product(grad_mlp_low[...], weights[block, :, down_columns])
        grad_hidden = to_half(grad_act * slopes[block].astype(jnp.float32))
        grad_hidden_low[block] = grad_hidden
        put_hidden(block).start()
        mlp_sum[...] += contract(grad_hidden, weights[block, :, up_columns], 1, 1)

    each_block(backward_mlp)

    def from_middle(group, rows):
        normed, inverse = normalize(middle[rows, :])
        grad_branch, grad_three, grad_four = normalize_back(
            normed, inverse, mod_row(mods_ref, 4, group), mlp_sum[rows, :]
        )
        grad_residual = grad_rows[rows, :] + grad_branch
        grad_mods_ref[1, pl.ds(group, 1), :] = grad_three
        grad_mods_ref[2, pl.ds(group, 1), :] = grad_four
        grad_mods_ref[0, pl.ds(group, 1), :] = jnp.sum(
            attn_sum[rows, :] * grad_residual, axis=0, keepdims=True
        )
        grad_rows[rows, :] = grad_residual
        grad_attn_low[rows, :] = to_half(mod_row(mods_ref, 2, group) * grad_residual)

    each_group(from_middle)
    put_grad_rows.start()
    put_grad_attn.start()

    def to_send(block):
        grad_mixed = to_half(product(grad_attn_low[...], weights[block, :, out_columns]))
        for place in range(per_block):
            send_ref[block * per_block + place] = grad_mixed[
                :, place * PAIR : (place + 1) * PAIR
            ]

    each_block(to_send)
    put_normed.wait()
    put_grad_mlp.wait()
    put_grad_rows.wait()
    put_grad_attn.wait()
    each_block(lambda block: put_act(block).wait())
    each_block(lambda block: put_hidden(block).wait())


def middle_layer(mixed_pairs, rows_in, mods, goal, coef, w_head, weights, head_cols, hidden_cols):
    blocks = weights.shape[0]
    tokens = rows_in.shape[0]
    groups = mods.shape[0]
    in_vmem = pl.BlockSpec(memory_space=pltpu.VMEM)
    in_hbm = pl.BlockSpec(memory_space=pl.ANY)
    rows_low = pltpu.VMEM((tokens, D), jnp.bfloat16)
    rows_full = pltpu.VMEM((tokens, D), jnp.float32)
    wide_low = pltpu.VMEM((blocks, tokens, hidden_cols), jnp.bfloat16)
    block_sems = pltpu.SemaphoreType.DMA((blocks,))
    return pl.pallas_call(
        partial(middle_kernel, head_cols, hidden_cols),
        in_specs=[in_vmem] * 6 + [in_hbm],
        out_specs=[in_hbm] * 6 + [in_vmem] * 4,
        out_shape=[
            jax.ShapeDtypeStruct((tokens, D), jnp.bfloat16),
            jax.ShapeDtypeStruct((tokens, blocks * hidden_cols), jnp.bfloat16),
            jax.ShapeDtypeStruct((tokens, D), jnp.bfloat16),
            jax.ShapeDtypeStruct((tokens, blocks * hidden_cols), jnp.bfloat16),
            jax.ShapeDtypeStruct((tokens, D), jnp.bfloat16),
            jax.ShapeDtypeStruct((tokens, D), jnp.float32),
            jax.ShapeDtypeStruct(mixed_pairs.shape, jnp.bfloat16),
            jax.ShapeDtypeStruct((6, groups, D), jnp.float32),
            jax.ShapeDtypeStruct(w_head.shape, jnp.float32),
            jax.ShapeDtypeStruct((8, PAIR), jnp.float32),
        ],
        scratch_shapes=[
            pltpu.VMEM(weights.shape, jnp.bfloat16),
            rows_low,
            wide_low,
            rows_low,
            wide_low,
            rows_low,
            rows_full,
            rows_full,
            rows_full,
            rows_full,
            wide_low,
            block_sems,
            block_sems,
            block_sems,
            block_sems,
            pltpu.SemaphoreType.DMA((4,)),
        ],
        cost_estimate=pl.CostEstimate(
            flops=4 * tokens * D * blocks * (2 * hidden_cols + head_cols),
            bytes_accessed=2 * weights.size + 30 * tokens * D,
            transcendentals=tokens * blocks * hidden_cols,
        ),
        compiler_params=pltpu.CompilerParams(vmem_limit_bytes=62 << 20),
    )(mixed_pairs, rows_in, mods, goal, coef, w_head, weights)


def close_kernel(
    blocks,
    grad_ref,
    rows_ref,
    grad_rows_ref,
    mods_ref,
    patch_ref,
    weight_ref,
    grad_mods_ref,
    grad_embed_ref,
    total,
):
    step = pl.program_id(0)
    groups = mods_ref.shape[0]
    rows_group = rows_ref.shape[0] // groups
    columns = grad_ref.shape[2]
    part = jnp.zeros(total.shape, jnp.float32)
    for place in range(grad_ref.shape[0]):
        part = part + contract(
            grad_ref[place], weight_ref[0, :, place * columns : (place + 1) * columns], 1, 1
        )

    @pl.when(step == 0)
    def first():
        total[...] = part

    @pl.when(step > 0)
    def later():
        total[...] += part

    @pl.when(step == blocks - 1)
    def finish():
        grad_embed_ref[...] = jnp.zeros_like(grad_embed_ref)

        def one_group(group, unused):
            rows = group_rows(group, rows_group)
            normed, inverse = normalize(rows_ref[rows, :])
            grad_branch, grad_zero, grad_one = normalize_back(
                normed, inverse, mod_row(mods_ref, 1, group), total[rows, :]
            )
            grad_mods_ref[0, pl.ds(group, 1), :] = grad_zero
            grad_mods_ref[1, pl.ds(group, 1), :] = grad_one
            grad_low = to_half(grad_rows_ref[rows, :] + grad_branch)
            grad_embed_ref[...] += contract(patch_ref[rows, :], grad_low, 0, 0)
            return unused

        lax.fori_loop(0, groups, one_group, 0)


def close_layer(grad_pairs, rows_in, grad_rows, mods, patch_rows, w_qkv):
    tokens = rows_in.shape[0]
    groups = mods.shape[0]
    blocks, unused, columns = w_qkv.shape
    per_block = columns // (3 * PAIR)

    def whole(shape):
        return pl.BlockSpec(shape, lambda step: (0,) * len(shape))

    return pl.pallas_call(
        partial(close_kernel, blocks),
        grid=(blocks,),
        in_specs=[
            pl.BlockSpec((per_block, tokens, 3 * PAIR), lambda step: (step, 0, 0)),
            whole(rows_in.shape),
            whole(grad_rows.shape),
            whole(mods.shape),
            whole(patch_rows.shape),
            pl.BlockSpec((1, D, columns), lambda step: (step, 0, 0)),
        ],
        out_specs=[whole((2, groups, D)), whole((PAIR, D))],
        out_shape=[
            jax.ShapeDtypeStruct((2, groups, D), jnp.float32),
            jax.ShapeDtypeStruct((PAIR, D), jnp.float32),
        ],
        scratch_shapes=[pltpu.VMEM((tokens, D), jnp.float32)],
        cost_estimate=pl.CostEstimate(
            flops=2 * tokens * D * blocks * columns,
            bytes_accessed=2 * blocks * D * columns + 16 * tokens * D,
            transcendentals=0,
        ),
        compiler_params=pltpu.CompilerParams(vmem_limit_bytes=60 << 20),
    )(grad_pairs, rows_in, grad_rows, mods, patch_rows, w_qkv)


def weight_kernel(clips, kinds, *refs):
    out = refs[-1]
    column = 0
    for kind in range(kinds):
        lefts = refs[2 * clips * kind : 2 * clips * kind + clips]
        rights = refs[2 * clips * kind + clips : 2 * clips * (kind + 1)]
        paired = len(rights[0].shape) == 3
        pieces = rights[0].shape[0] if paired else rights[0].shape[1] // 512
        width = rights[0].shape[2] if paired else 512
        for piece in range(pieces):
            total = None
            for left, right in zip(lefts, rights):
                block = right[piece] if paired else right[:, piece * width : (piece + 1) * width]
                part = contract(left[...], block, 0, 0)
                total = part if total is None else total + part
            out[0, :, column : column + width] = to_half(total)
            column += width


def weight_grads(blocks, terms):
    clips = len(terms[0][0])
    operands = []
    specs = []
    columns_all = 0
    flops = 0
    for lefts, rights in terms:
        for left in lefts:
            operands.append(left)
            specs.append(pl.BlockSpec(left.shape, lambda step: (0, 0)))
        for right in rights:
            operands.append(right)
            if right.ndim == 3:
                per_block = right.shape[0] // blocks
                specs.append(
                    pl.BlockSpec((per_block,) + right.shape[1:], lambda step: (step, 0, 0))
                )
                columns = per_block * right.shape[2]
            else:
                columns = right.shape[1] // blocks
                specs.append(pl.BlockSpec((right.shape[0], columns), lambda step: (0, step)))
            flops += 2 * right.size * D
        columns_all += columns
    return pl.pallas_call(
        partial(weight_kernel, clips, len(terms)),
        grid=(blocks,),
        in_specs=specs,
        out_specs=pl.BlockSpec((1, D, columns_all), lambda step: (step, 0, 0)),
        out_shape=jax.ShapeDtypeStruct((blocks, D, columns_all), jnp.bfloat16),
        cost_estimate=pl.CostEstimate(
            flops=flops,
            bytes_accessed=2 * blocks * D * columns_all + 2 * sum(op.size for op in operands),
            transcendentals=0,
        ),
        compiler_params=pltpu.CompilerParams(vmem_limit_bytes=62 << 20),
    )(*operands)


def pack_kernel(head_cols, in_ref, outs_ref, qkv_ref, rest_ref):
    pairs = head_cols // PAIR
    for pair in range(pairs):
        for kind in range(3):
            source = (kind * pairs + pair) * PAIR
            place = (pair * 3 + kind) * PAIR
            qkv_ref[:, place : place + PAIR] = to_half(in_ref[:, source : source + PAIR])
    hidden_cols = in_ref.shape[1] - 3 * head_cols
    rest_ref[:, :hidden_cols] = to_half(in_ref[:, 3 * head_cols :])
    columns = to_half(outs_ref[...].T)
    rest_ref[:, hidden_cols : 2 * hidden_cols] = columns[:, head_cols:]
    rest_ref[:, 2 * hidden_cols :] = columns[:, :head_cols]


def pack_weights(w_in, w_outs, head_cols):
    rows = w_in.shape[0]
    hidden_cols = w_in.shape[1] - 3 * head_cols
    return pl.pallas_call(
        partial(pack_kernel, head_cols),
        out_shape=[
            jax.ShapeDtypeStruct((rows, 3 * head_cols), jnp.bfloat16),
            jax.ShapeDtypeStruct((rows, 2 * hidden_cols + head_cols), jnp.bfloat16),
        ],
    )(w_in, w_outs)


def swap_groups(array_in):
    dp_size = lax.axis_size("dp")
    tensor_size = lax.axis_size("tensor")
    pairs = [
        (row * tensor_size + column, column * dp_size + row)
        for row in range(dp_size)
        for column in range(tensor_size)
    ]
    return lax.ppermute(array_in, ("dp", "tensor"), pairs)


MESH_ID = pl.DeviceIdType.MESH


def places():
    dp_size, frame_size, tensor_size = [
        lax.axis_size(axis) for axis in ("dp", "frame", "tensor")
    ]
    here = [lax.axis_index(axis) for axis in ("dp", "frame", "tensor")]
    return (dp_size, frame_size, tensor_size, *here)


def device(row, frame, column):
    return {"dp": row, "frame": frame, "tensor": column}


def greet_plane():
    dp_size, frame_size, tensor_size, row, frame, column = places()
    plane = dp_size * frame_size
    barrier = pltpu.get_barrier_semaphore()
    for shift in range(1, plane):
        other = lax.rem(row * frame_size + frame + shift, plane)
        pl.semaphore_signal(
            barrier,
            inc=1,
            device_id=device(lax.div(other, frame_size), lax.rem(other, frame_size), column),
            device_id_type=MESH_ID,
        )
    pl.semaphore_wait(barrier, plane - 1)


def greet_all():
    dp_size, frame_size, tensor_size, row, frame, column = places()
    plane = dp_size * frame_size
    everyone = plane * tensor_size
    here = (row * frame_size + frame) * tensor_size + column
    barrier = pltpu.get_barrier_semaphore()

    def signal(shift, unused):
        other = lax.rem(here + shift, everyone)
        place = lax.div(other, tensor_size)
        pl.semaphore_signal(
            barrier,
            inc=1,
            device_id=device(
                lax.div(place, frame_size), lax.rem(place, frame_size), lax.rem(other, tensor_size)
            ),
            device_id_type=MESH_ID,
        )
        return unused

    lax.fori_loop(1, everyone, signal, 0)
    pl.semaphore_wait(barrier, everyone - 1)


def send(source, target, send_sem, receive_sem, device_id):
    return pltpu.make_async_remote_copy(
        src_ref=source,
        dst_ref=target,
        send_sem=send_sem,
        recv_sem=receive_sem,
        device_id=device_id,
        device_id_type=MESH_ID,
    )


def plane_copies(source_of, target_of, send_sems, receive_sems):
    dp_size, frame_size, tensor_size, row, frame, column = places()
    plane = dp_size * frame_size
    here = row * frame_size + frame
    copies = []
    for shift in range(1, plane):
        other = lax.rem(here + shift, plane)
        copies.append(
            send(
                source_of(other),
                target_of(here),
                send_sems.at[shift - 1],
                receive_sems.at[shift - 1],
                device(lax.div(other, frame_size), lax.rem(other, frame_size), column),
            )
        )
    return copies


def axis_copies(axis, source_of, target_of, send_sems, receive_sems):
    size = lax.axis_size(axis)
    here = lax.axis_index(axis)
    row, frame, column = [lax.axis_index(name) for name in ("dp", "frame", "tensor")]
    copies = []
    for shift in range(1, size):
        other = lax.rem(here + shift, size)
        target = device(other, frame, column) if axis == "dp" else device(row, frame, other)
        copies.append(
            send(
                source_of(other),
                target_of(here),
                send_sems.at[shift - 1],
                receive_sems.at[shift - 1],
                target,
            )
        )
    return copies


def plane_gather_kernel(count, *refs):
    ins = refs[:count]
    outs = refs[count : 2 * count]
    sems = refs[2 * count :]
    greet_plane()
    here = lax.axis_index("dp") * lax.axis_size("frame") + lax.axis_index("frame")
    copies = []
    for place in range(count):
        copies += plane_copies(
            lambda other, place=place: ins[place],
            lambda own, place=place: outs[place].at[own],
            sems[2 * place],
            sems[2 * place + 1],
        )
    for copy in copies:
        copy.start()
    for place in range(count):
        outs[place][here] = ins[place][...]
    for copy in copies:
        copy.wait()


def remote_call(kernel, collective_id, out_shape, scratch_shapes, operands):
    in_vmem = pl.BlockSpec(memory_space=pltpu.VMEM)
    return pl.pallas_call(
        kernel,
        out_shape=out_shape,
        in_specs=[in_vmem] * len(operands),
        out_specs=[in_vmem] * len(out_shape),
        scratch_shapes=scratch_shapes,
        compiler_params=pltpu.CompilerParams(
            collective_id=collective_id, has_side_effects=True, vmem_limit_bytes=48 << 20
        ),
    )(*operands)


def plane_gather(arrays):
    plane = lax.axis_size("dp") * lax.axis_size("frame")
    return remote_call(
        partial(plane_gather_kernel, len(arrays)),
        0,
        [jax.ShapeDtypeStruct((plane,) + array.shape, array.dtype) for array in arrays],
        [pltpu.SemaphoreType.DMA((plane - 1,))] * (2 * len(arrays)),
        arrays,
    )


def swap_block(block, swapped, send_sem, receive_sem, start):
    row, frame, column = [lax.axis_index(name) for name in ("dp", "frame", "tensor")]
    own = row == column
    copy = send(block, swapped, send_sem, receive_sem, device(column, frame, row))

    @pl.when(jnp.logical_not(own))
    def remote():
        copy.start() if start else copy.wait()

    if start:

        @pl.when(own)
        def keep():
            swapped[...] = block[...]


def mods_kernel(
    parts,
    out,
    received,
    block,
    swapped,
    plane_send,
    plane_receive,
    swap_send,
    swap_receive,
    spread_send,
    spread_receive,
):
    dp_size, frame_size, tensor_size, row, frame, column = places()
    plane = dp_size * frame_size
    here = row * frame_size + frame
    greet_all()
    copies = plane_copies(
        lambda other: parts.at[other], lambda own: received.at[own], plane_send, plane_receive
    )
    for copy in copies:
        copy.start()
    received[here] = parts[here]
    for copy in copies:
        copy.wait()
    total = received[0]
    for place in range(1, plane):
        total = total + received[place]
    block[...] = total
    swap_block(block, swapped, swap_send.at[0], swap_receive.at[0], True)
    swap_block(block, swapped, swap_send.at[0], swap_receive.at[0], False)
    copies = axis_copies(
        "dp", lambda other: swapped, lambda own: out.at[own], spread_send, spread_receive
    )
    for copy in copies:
        copy.start()
    out[row] = swapped[...]
    for copy in copies:
        copy.wait()


def spread_mods(parts):
    plane, rows, columns = parts.shape
    dma = pltpu.SemaphoreType.DMA
    dp_size = lax.axis_size("dp")
    return remote_call(
        mods_kernel,
        1,
        [jax.ShapeDtypeStruct((dp_size, rows, columns), jnp.float32)],
        [
            pltpu.VMEM(parts.shape, jnp.float32),
            pltpu.VMEM(parts.shape[1:], jnp.float32),
            pltpu.VMEM(parts.shape[1:], jnp.float32),
            dma((plane - 1,)),
            dma((plane - 1,)),
            dma((1,)),
            dma((1,)),
            dma((dp_size - 1,)),
            dma((dp_size - 1,)),
        ],
        [parts],
    )[0]


def cond_kernel(
    mod_parts,
    patch_parts,
    weight,
    mod_all,
    cond_all,
    patch_out,
    mod_received,
    patch_received,
    mod_block,
    patch_block,
    patch_tensor,
    cond_part,
    cond_tensor,
    mod_swapped,
    cond_block,
    swap_send,
    swap_receive,
    dp_send,
    dp_receive,
    patch_send,
    patch_receive,
    spread_send,
    spread_receive,
    patch_tensor_send,
    patch_tensor_receive,
    cond_send,
    cond_receive,
    gather_send,
    gather_receive,
):
    dp_size, frame_size, tensor_size, row, frame, column = places()
    plane = dp_size * frame_size
    here = row * frame_size + frame
    greet_all()
    copies = axis_copies(
        "dp",
        lambda other: mod_parts.at[other],
        lambda own: mod_received.at[own],
        dp_send,
        dp_receive,
    ) + plane_copies(
        lambda other: patch_parts.at[other],
        lambda own: patch_received.at[own],
        patch_send,
        patch_receive,
    )
    for copy in copies:
        copy.start()
    mod_received[row] = mod_parts[row]
    patch_received[here] = patch_parts[here]
    for copy in copies:
        copy.wait()
    total = mod_received[0]
    for place in range(1, dp_size):
        total = total + mod_received[place]
    mod_block[...] = to_half(total)
    total = patch_received[0]
    for place in range(1, plane):
        total = total + patch_received[place]
    patch_block[...] = total
    swap_block(mod_block, mod_swapped, swap_send.at[0], swap_receive.at[0], True)
    patch_copies = axis_copies(
        "tensor",
        lambda other: patch_block,
        lambda own: patch_tensor.at[own],
        patch_tensor_send,
        patch_tensor_receive,
    )
    for copy in patch_copies:
        copy.start()
    patch_tensor[column] = patch_block[...]
    swap_block(mod_block, mod_swapped, swap_send.at[0], swap_receive.at[0], False)
    mod_copies = plane_copies(
        lambda other: mod_swapped, lambda own: mod_all.at[own], spread_send, spread_receive
    )
    cond_part[...] = contract(mod_swapped[...], weight[...], 1, 1)
    cond_copies = axis_copies(
        "tensor",
        lambda other: cond_part,
        lambda own: cond_tensor.at[own],
        cond_send,
        cond_receive,
    )
    for copy in cond_copies + mod_copies:
        copy.start()
    mod_all[here] = mod_swapped[...]
    cond_tensor[column] = cond_part[...]
    for copy in patch_copies + cond_copies:
        copy.wait()
    total = cond_tensor[0]
    total_patch = patch_tensor[0]
    for place in range(1, tensor_size):
        total = total + cond_tensor[place]
        total_patch = total_patch + patch_tensor[place]
    patch_out[...] = total_patch
    cond_block[...] = total
    gather_copies = plane_copies(
        lambda other: cond_block, lambda own: cond_all.at[own], gather_send, gather_receive
    )
    for copy in gather_copies:
        copy.start()
    cond_all[here] = total
    for copy in gather_copies + mod_copies:
        copy.wait()


def cond_sums(mod_parts, patch_parts, weight):
    dp_size, rows, columns = mod_parts.shape
    plane = patch_parts.shape[0]
    tensor_size = lax.axis_size("tensor")
    features = weight.shape[0]

    def held(*shape):
        return pltpu.VMEM(shape, jnp.float32)

    def sems(*counts):
        return [pltpu.SemaphoreType.DMA((count,)) for count in counts]

    patch_shape = patch_parts.shape[1:]
    return remote_call(
        cond_kernel,
        2,
        [
            jax.ShapeDtypeStruct((plane, rows, columns), jnp.bfloat16),
            jax.ShapeDtypeStruct((plane, rows, features), jnp.float32),
            jax.ShapeDtypeStruct(patch_shape, jnp.float32),
        ],
        [
            held(*mod_parts.shape),
            held(*patch_parts.shape),
            pltpu.VMEM((rows, columns), jnp.bfloat16),
            held(*patch_shape),
            held(tensor_size, *patch_shape),
            held(rows, features),
            held(tensor_size, rows, features),
            pltpu.VMEM((rows, columns), jnp.bfloat16),
            held(rows, features),
        ]
        + sems(1, 1, dp_size - 1, dp_size - 1, *[plane - 1] * 4)
        + sems(*[tensor_size - 1] * 4, plane - 1, plane - 1),
        [mod_parts, patch_parts, weight],
    )


def total_kernel(tile, out, received, send_sems, receive_sems):
    dp_size, frame_size, tensor_size, row, frame, column = places()
    everyone = dp_size * frame_size * tensor_size
    here = (row * frame_size + frame) * tensor_size + column
    greet_all()

    def copy_to(shift):
        other = lax.rem(here + shift, everyone)
        place = lax.div(other, tensor_size)
        return send(
            tile,
            received.at[here],
            send_sems.at[shift - 1],
            receive_sems.at[shift - 1],
            device(
                lax.div(place, frame_size), lax.rem(place, frame_size), lax.rem(other, tensor_size)
            ),
        )

    def start(shift, unused):
        copy_to(shift).start()
        return unused

    def finish(shift, unused):
        copy_to(shift).wait()
        return unused

    lax.fori_loop(1, everyone, start, 0)
    received[here] = tile[...]
    lax.fori_loop(1, everyone, finish, 0)
    out[...] = jnp.sum(received[...], axis=0)


def total_over_all(first, second):
    lane = jnp.arange(PAIR)[None, :]
    tile = jnp.where(lane == 0, first, jnp.where(lane == 1, second, 0.0))
    tile = jnp.broadcast_to(tile, (8, PAIR)).astype(jnp.float32)
    everyone = lax.axis_size(EVERY)
    sums = remote_call(
        total_kernel,
        3,
        [jax.ShapeDtypeStruct((8, PAIR), jnp.float32)],
        [
            pltpu.VMEM((everyone, 8, PAIR), jnp.float32),
            pltpu.SemaphoreType.DMA((everyone - 1,)),
            pltpu.SemaphoreType.DMA((everyone - 1,)),
        ],
        [tile],
    )[0]
    return (sums[0, 0], sums[0, 1])


def spread_heads():
    return (D // PAIR) % (lax.axis_size("dp") * lax.axis_size("frame")) == 0


def exchange_axes():
    axes = PLANE if spread_heads() else ("dp",)
    return (axes, math.prod(lax.axis_size(axis) for axis in axes))


def to_heads(pairs_in):
    axes, parts = exchange_axes()
    pairs, tokens, columns = pairs_in.shape
    moved = lax.all_to_all(
        pairs_in.reshape(parts, pairs // parts, tokens, columns), axes, 0, 0, tiled=True
    )
    return jnp.swapaxes(moved, 0, 1).reshape(pairs // parts, parts * tokens, columns)


def to_tokens(units_in):
    axes, parts = exchange_axes()
    units, tokens_all, columns = units_in.shape
    by_place = jnp.swapaxes(units_in.reshape(units, parts, tokens_all // parts, columns), 0, 1)
    moved = lax.all_to_all(by_place, axes, 0, 0, tiled=True)
    return moved.reshape(parts * units, tokens_all // parts, columns)


def gather_blocks(shard):
    whole = lax.all_gather(shard, EVERY, axis=0, tiled=True)
    return whole.reshape(lax.axis_size("tensor"), D, -1)


def scatter_blocks(blocks_in):
    flat = blocks_in.reshape(-1, blocks_in.shape[-1])
    return lax.psum_scatter(flat, EVERY, scatter_dimension=0, tiled=True)


def pad_lanes(rows_in, axis):
    widths = [(0, 0)] * rows_in.ndim
    widths[axis] = (0, PAIR - rows_in.shape[axis])
    return jnp.pad(rows_in, widths)


def after(value, *others):
    return lax.optimization_barrier((value,) + others)[0]


def update_part(refs, rows, columns, gradient, rates):
    master_ref, first_ref, second_ref, master_out, first_out, second_out, half_out = refs
    factor, fix_first, fix_second = rates
    place = (Ellipsis, rows, columns)
    master = master_ref[place]
    clipped = gradient * factor
    first_new = BETA_FIRST * first_ref[place] + (1.0 - BETA_FIRST) * clipped
    second_new = BETA_SECOND * second_ref[place] + (1.0 - BETA_SECOND) * clipped * clipped
    step_dir = first_new / fix_first / (jnp.sqrt(second_new / fix_second) + ADAM_EPS)
    master_new = master - LEARN_RATE * (step_dir + WEIGHT_DECAY * master)
    master_out[place] = master_new
    first_out[place] = first_new
    second_out[place] = second_new
    half_out[place] = to_half(master_new)


def update_kernel(head_cols, rates_ref, qkv_ref, rest_ref, cond_ref, time_ref, patch_ref, *refs):
    rates = (rates_ref[0], rates_ref[1], rates_ref[2])
    sets = [refs[which::5] for which in range(5)]
    everything = slice(None)
    pairs = head_cols // PAIR
    for pair in range(pairs):
        for kind in range(3):
            source = (pair * 3 + kind) * PAIR
            place = (kind * pairs + pair) * PAIR
            update_part(
                sets[0],
                everything,
                slice(place, place + PAIR),
                qkv_ref[:, source : source + PAIR].astype(jnp.float32),
                rates,
            )
    qkv_cols = 3 * head_cols
    hidden_cols = sets[0][0].shape[1] - qkv_cols
    for start in range(0, hidden_cols, 256):
        update_part(
            sets[0],
            everything,
            slice(qkv_cols + start, qkv_cols + start + 256),
            rest_ref[:, start : start + 256].astype(jnp.float32),
            rates,
        )
    for start in range(0, hidden_cols + head_cols, 256):
        source = 2 * hidden_cols if start == 0 else hidden_cols + start - head_cols
        gradient = rest_ref[:, source : source + 256].astype(jnp.float32).T
        update_part(sets[1], slice(start, start + 256), everything, gradient, rates)
    for start in range(0, cond_ref.shape[1], 256):
        columns = slice(start, start + 256)
        update_part(sets[2], everything, columns, cond_ref[:, columns], rates)
    for start in range(0, D, 256):
        columns = slice(start, start + 256)
        update_part(sets[3], everything, columns, time_ref[:, columns], rates)
    update_part(sets[4], everything, everything, patch_ref[...], rates)


def update_all(rates, gradients, masters, firsts, seconds, head_cols):
    operands = list(gradients) + list(masters) + list(firsts) + list(seconds)
    shapes = [master.shape for master in masters]
    in_vmem = pl.BlockSpec(memory_space=pltpu.VMEM)
    return pl.pallas_call(
        partial(update_kernel, head_cols),
        in_specs=[pl.BlockSpec(memory_space=pltpu.SMEM)] + [in_vmem] * len(operands),
        out_specs=[in_vmem] * 20,
        out_shape=[jax.ShapeDtypeStruct(shape, jnp.float32) for shape in shapes] * 3
        + [jax.ShapeDtypeStruct(shape, jnp.bfloat16) for shape in shapes],
        compiler_params=pltpu.CompilerParams(vmem_limit_bytes=60 << 20),
    )(rates, *operands)


def shards(
    latent,
    noise_draw,
    levels,
    context,
    step_count,
    w_in,
    w_outs,
    w_cond,
    w_time,
    w_patch,
    m_in,
    m_outs,
    m_cond,
    m_time,
    m_patch,
    v_in,
    v_outs,
    v_cond,
    v_time,
    v_patch,
):
    head_cols = D // lax.axis_size("tensor")
    pairs_block = head_cols // PAIR
    pairs_all = D // PAIR
    masters = (w_in, w_outs, w_cond, w_time, w_patch)
    clips, frames_here, patch_rows, width = latent.shape
    groups = clips * frames_here
    plane_index = lax.axis_index(PLANE)
    half_cond, half_time, half_patch = [to_half(m) for m in masters[2:]]
    hidden_cols = w_in.shape[1] - 3 * head_cols
    shard_qkv, shard_rest = pack_weights(w_in, w_outs, head_cols)

    w_qkv = gather_blocks(shard_qkv)
    level_rows = jnp.pad(
        levels.astype(jnp.float32), ((0, 8 - clips), (0, PAIR - frames_here))
    )
    time_places, patch_places, level_places = plane_gather([half_time, half_patch, level_rows])
    time_whole = time_places.reshape(-1, D)
    patch_whole = jnp.moveaxis(patch_places, 0, 2).reshape(2, PD, D)
    fields = swap_groups(jnp.stack([latent, noise_draw]))
    levels_all = level_places[:, :clips, :frames_here]
    blocks = lax.axis_size("tensor")
    w_first = time_whole[:TEMB]
    w_second = time_whole[TEMB:]
    w_embed = pad_lanes(patch_whole[0], 0)
    w_head = pad_lanes(patch_whole[1], 0)

    token_total = (TOKF * jnp.sum(FRAMES - context)).astype(jnp.float32)
    dp_size = lax.axis_size("dp")
    frame_size = lax.axis_size("frame")
    clip_ids = jnp.arange(dp_size * clips, dtype=jnp.int32).reshape(dp_size, 1, clips, 1)
    frame_ids = jnp.arange(FRAMES, dtype=jnp.int32).reshape(1, frame_size, 1, frames_here)
    clean_all = frame_ids < context[clip_ids]
    level_all = jnp.where(
        clean_all, 0.0, levels_all.reshape(dp_size, frame_size, clips, frames_here)
    )
    embed_low = to_half(frequency_table(level_all.reshape(-1)))
    hidden_time = product(embed_low, w_first)
    first_low = to_half(jax.nn.silu(hidden_time))
    cond_vec = product(first_low, w_second)
    cond_low = to_half(jax.nn.silu(cond_vec))
    frame_index = lax.axis_index("frame")
    tensor_index = lax.axis_index("tensor")
    cond_rows = half_cond.shape[0]
    cond_own = lax.dynamic_slice_in_dim(cond_low, plane_index * cond_rows, cond_rows, 1)
    mod_parts = product(cond_own, half_cond).reshape(dp_size * frame_size, groups, -1)
    def own_part(whole):
        part = lax.dynamic_index_in_dim(whole, tensor_index, 0, keepdims=False)
        return lax.dynamic_index_in_dim(part, frame_index, 0, keepdims=False)

    clean_frames = own_part(clean_all)
    alpha_coef, sigma_coef = noise_terms(own_part(level_all))
    alpha_field = alpha_coef[:, :, None, None]
    sigma_field = sigma_coef[:, :, None, None]
    clean_field = fields[0].astype(jnp.float32)
    noise_field = fields[1].astype(jnp.float32)
    noisy_field = alpha_field * clean_field + sigma_field * noise_field
    target = alpha_field * noise_field - sigma_field * clean_field
    patch_low = pad_lanes(to_half(patchify(noisy_field).reshape(clips, -1, PD)), 2)
    goal_rows = pad_lanes(patchify(target).reshape(clips, -1, PD), 2)
    coef = (1.0 - clean_frames.astype(jnp.float32)) / token_total
    coef_rows = jnp.broadcast_to(coef[:, :, None], (clips, frames_here, PAIR))


    mod_parts, patch_low, goal_rows, coef_rows = lax.optimization_barrier(
        (mod_parts, patch_low, goal_rows, coef_rows)
    )
    modulation = jnp.swapaxes(spread_mods(mod_parts), 0, 1)
    mods = modulation.reshape(clips, frames_here, -1)

    spread = spread_heads()
    each_clip = range(clips)
    opened = [
        open_layer(patch_low[clip], w_embed, mods[clip], w_qkv) for clip in each_clip
    ]
    rows_in = [parts[0] for parts in opened]
    flat_one = [parts[1] for parts in opened]
    kept = []
    mixed_pairs = []
    mixed_lows = []
    for clip in each_clip:
        qkv_send = opened[clip][2]
        if clip > 1:
            qkv_send = after(qkv_send, mixed_lows[clip - 2])
        qkv_heads = to_heads(qkv_send)
        if clip == 0:
            w_rest = gather_blocks(after(shard_rest, qkv_heads, *rows_in[1:]))
            cond_whole = lax.all_gather(after(half_cond, w_rest), PLANE, axis=0, tiled=True)
        else:
            qkv_heads = after(qkv_heads, mixed_lows[clip - 1])
        if spread:
            key_value, key_place = qkv_heads, 1
        else:
            key_value = lax.all_gather(qkv_heads[..., PAIR:], "frame", axis=1, tiled=True)
            key_place = 0
        exps, mixed_low, mixed, inverse = attend(qkv_heads, key_value, key_place)
        kept.append((exps, qkv_heads, key_value, key_place, mixed, inverse))
        mixed_lows.append(mixed_low)
    middles = []
    grad_heads = []
    for clip in each_clip:
        gates = mixed_lows[clip + 1 : clip + 2]
        if not gates and clip > 1:
            gates = [middles[clip - 2][5]]
        mixed_pairs.append(to_tokens(after(mixed_lows[clip], *gates)))
        middles.append(
            middle_layer(
                mixed_pairs[clip],
                rows_in[clip],
                mods[clip],
                goal_rows[clip],
                coef_rows[clip],
                w_head,
                w_rest,
                head_cols,
                hidden_cols,
            )
        )
    flat_two, act_low, grad_mlp, grad_hidden, grad_attn, grad_rows = [
        [parts[place] for parts in middles] for place in range(6)
    ]
    loss_part = sum(jnp.sum(parts[9]) for parts in middles)
    grad_head = sum(parts[8][:PD] for parts in middles)
    grad_heads = [to_heads(after(middles[0][6], middles[1 % clips][5]))]
    flat_two[-1] = after(flat_two[-1], *grad_heads)
    grad_rest = weight_grads(
        blocks,
        [(flat_two, grad_hidden), (grad_mlp, act_low), (grad_attn, mixed_pairs)],
    )
    scattered_rest = scatter_blocks(after(grad_rest, cond_whole))
    if clips > 1:
        sends = after(jnp.concatenate([parts[6] for parts in middles[1:]], axis=1), grad_rest)
        together = to_heads(sends).reshape(
            kept[0][5].shape[0], -1, clips - 1, sends.shape[1] // (clips - 1), PAIR
        )
        grad_heads += [
            together[:, :, clip].reshape(together.shape[0], -1, PAIR) for clip in range(clips - 1)
        ]
    grad_pairs = []
    for clip in each_clip:
        exps, qkv_heads, key_value, key_place, mixed, inverse = kept[clip]
        grad_now = after(grad_heads[clip], grad_rest)
        if clip > 1:
            grad_now = after(grad_now, grad_pairs[clip - 2])
        grads = attend_back(exps, qkv_heads, key_value, key_place, grad_now, mixed, inverse)
        if not spread:
            grads = [grads[0]] + [
                lax.psum_scatter(grad, "frame", scatter_dimension=1, tiled=True)
                for grad in grads[1:]
            ]
        grad_units = grads[0] if len(grads) == 1 else jnp.concatenate(grads, axis=-1)
        grad_pairs.append(to_tokens(grad_units))
    closed = []
    for clip in each_clip:
        if clip == clips - 1:
            grad_pairs[clip] = after(
                grad_pairs[clip], scattered_rest, *[parts[0] for parts in closed]
            )
            grad_wqkv = weight_grads(blocks, [(flat_one, grad_pairs)])
            scattered_qkv = scatter_blocks(grad_wqkv)
            grad_pairs[clip] = after(grad_pairs[clip], grad_wqkv)
        closed.append(
            close_layer(
                grad_pairs[clip], rows_in[clip], grad_rows[clip], mods[clip], patch_low[clip], w_qkv
            )
        )
    grad_embed = sum(parts[1][:PD] for parts in closed)
    patch_cols = half_patch.shape[2]
    patch_parts = jnp.swapaxes(
        jnp.concatenate([grad_embed, grad_head], axis=0).reshape(2 * PD, -1, patch_cols), 0, 1
    )
    grad_mod = jnp.stack(
        [jnp.concatenate([closed[clip][0], middles[clip][7]], axis=0) for clip in each_clip]
    )
    mod_parts = jnp.transpose(
        grad_mod.reshape(clips, dp_size, -1, frames_here, D), (1, 0, 3, 2, 4)
    ).reshape(dp_size, groups, -1)
    mod_all, cond_places, patch_block = cond_sums(mod_parts, patch_parts, cond_whole)
    mod_all = mod_all.reshape(-1, mod_all.shape[-1])
    grad_cond_all = cond_places.reshape(-1, D)
    final_patch = patch_block.reshape(2, PD, patch_cols)
    final_cond = rows_product(cond_own, mod_all)
    unused, silu_cond = jax.vjp(jax.nn.silu, cond_vec)
    grad_cond_low = to_half(silu_cond(grad_cond_all)[0])
    grad_second = rows_product(first_low, grad_cond_low)
    grad_first_act = cols_product(grad_cond_low, w_second)
    unused, silu_first = jax.vjp(jax.nn.silu, hidden_time)
    grad_hidden_time = to_half(silu_first(grad_first_act)[0])
    grad_first = rows_product(embed_low, grad_hidden_time)
    time_rows = half_time.shape[0]
    final_time = lax.dynamic_slice_in_dim(
        jnp.concatenate([grad_first, grad_second], axis=0), plane_index * time_rows, time_rows, 0
    )
    def square_sum(gradient):
        wide = gradient.astype(jnp.float32)
        return jnp.sum(wide * wide)

    split_square = sum(square_sum(part) for part in (scattered_qkv, scattered_rest, final_cond))
    shared_square = (square_sum(final_time) + square_sum(final_patch)) / blocks
    totals = total_over_all(loss_part, split_square + shared_square)
    loss_value = totals[0]
    grad_norm = jnp.sqrt(totals[1])
    factor = jnp.minimum(1.0, MAX_NORM / (grad_norm + 1e-06))
    steps_done = step_count[0].astype(jnp.float32)
    fix_first = 1.0 - BETA_FIRST**steps_done
    fix_second = 1.0 - BETA_SECOND**steps_done
    results = update_all(
        jnp.stack([factor, fix_first, fix_second]),
        (scattered_qkv, scattered_rest, final_cond, final_time, final_patch),
        masters,
        (m_in, m_outs, m_cond, m_time, m_patch),
        (v_in, v_outs, v_cond, v_time, v_patch),
        head_cols,
    )
    return (loss_value, grad_norm, *results)


def solution(mesh):
    placed = (
        P("dp", "frame", "tensor", None),
        P("dp", "frame", "tensor", None),
        P("dp", "frame"),
        P(),
        P(),
        P(("dp", "frame"), "tensor"),
        P("tensor", ("dp", "frame")),
        P(("dp", "frame"), "tensor"),
        P(("dp", "frame"), None),
        P(None, None, ("dp", "frame")),
        P(("dp", "frame"), "tensor"),
        P("tensor", ("dp", "frame")),
        P(("dp", "frame"), "tensor"),
        P(("dp", "frame"), None),
        P(None, None, ("dp", "frame")),
        P(("dp", "frame"), "tensor"),
        P("tensor", ("dp", "frame")),
        P(("dp", "frame"), "tensor"),
        P(("dp", "frame"), None),
        P(None, None, ("dp", "frame")),
    )
    return jax.shard_map(
        shards,
        mesh=mesh,
        in_specs=placed,
        out_specs=(
            P(),
            P(),
            P(("dp", "frame"), "tensor"),
            P("tensor", ("dp", "frame")),
            P(("dp", "frame"), "tensor"),
            P(("dp", "frame"), None),
            P(None, None, ("dp", "frame")),
            P(("dp", "frame"), "tensor"),
            P("tensor", ("dp", "frame")),
            P(("dp", "frame"), "tensor"),
            P(("dp", "frame"), None),
            P(None, None, ("dp", "frame")),
            P(("dp", "frame"), "tensor"),
            P("tensor", ("dp", "frame")),
            P(("dp", "frame"), "tensor"),
            P(("dp", "frame"), None),
            P(None, None, ("dp", "frame")),
            P(("dp", "frame"), "tensor"),
            P("tensor", ("dp", "frame")),
            P(("dp", "frame"), "tensor"),
            P(("dp", "frame"), None),
            P(None, None, ("dp", "frame")),
        ),
        check_vma=False,
    )
```

profile of v0, /device:TPU:0, one launch (start us, length us, event | category | flops | bytes accessed | tf_op | source)
XLA Modules:
  0.0 966.2 jit_solution(9713273754867142003)
XLA Ops:
  17.3 44.9 %shard_map.363 = (bf16[8,160,1024]{2,1,0:T(8,128)(2,1)S(1)}, bf16[8,2,16,128]{3,2,1,0:T(8,128)(2,1)S(1)}, f32[8,8,128]{2,1,0:T(8,128)S(1)}) custom-call(bf16[160,1024]{1,0:T(8,128)(2,1)S(1)} %convert_element_type.80.refs_0_, bf16[2,16,128]{2,1,0:T(8,128)(2,1)S(1)} %convert_element_type.81.refs_1_, f32[8,128]{1,0:T(8,128)S(1)} %pad.19.refs_2_), custom_call_target="tpu_custom_call" | custom-call | tf_op jit(solution)/shard_map/pallas_call | solution.py:976
  77.9 38.2 %shard_map.364 = f32[4,24,2048]{2,1,0:T(8,128)S(1)} custom-call(f32[8,24,2048]{2,1,0:T(8,128)S(1)} %bitcast.147), custom_call_target="tpu_custom_call" | custom-call | tf_op jit(solution)/shard_map/pallas_call | solution.py:976
  117.8 11.3 %shard_map.366 = (f32[512,1024]{1,0:T(8,128)}, bf16[512,1024]{1,0:T(8,128)(2,1)}, bf16[8,512,384]{2,1,0:T(8,128)(2,1)}) custom-call(bf16[512,128]{1,0:T(8,128)(2,1)} %get-tuple-element.250.patch_ref, bf16[128,1024]{1,0:T(8,128)(2,1)} %pad.22.embed_ref, f32[8,8192]{1,0:T(8,128)} %bitcast.193, bf16[4,1024,768]{2,1,0:T(8,128)(2,1)} %bitcast.156), custom_call_target="tpu_custom_call" | custom-call | flops 3221225472 | bytes 12582912 | tf_op jit(solution)/shard_map/pallas_call | solution.py:382
  132.8 11.3 %shard_map.368 = (f32[512,1024]{1,0:T(8,128)}, bf16[512,1024]{1,0:T(8,128)(2,1)}, bf16[8,512,384]{2,1,0:T(8,128)(2,1)}) custom-call(bf16[512,128]{1,0:T(8,128)(2,1)} %get-tuple-element.249.patch_ref, bf16[128,1024]{1,0:T(8,128)(2,1)} %pad.22.embed_ref, f32[8,8192]{1,0:T(8,128)} %bitcast.190, bf16[4,1024,768]{2,1,0:T(8,128)(2,1)} %bitcast.157), custom_call_target="tpu_custom_call" | custom-call | flops 3221225472 | bytes 12582912 | tf_op jit(solution)/shard_map/pallas_call | solution.py:382
  144.1 11.4 %shard_map.370 = (f32[512,1024]{1,0:T(8,128)}, bf16[512,1024]{1,0:T(8,128)(2,1)}, bf16[8,512,384]{2,1,0:T(8,128)(2,1)}) custom-call(bf16[512,128]{1,0:T(8,128)(2,1)} %get-tuple-element.248.patch_ref, bf16[128,1024]{1,0:T(8,128)(2,1)} %pad.22.embed_ref, f32[8,8192]{1,0:T(8,128)} %bitcast.187, bf16[4,1024,768]{2,1,0:T(8,128)(2,1)} %bitcast.158), custom_call_target="tpu_custom_call" | custom-call | flops 3221225472 | bytes 12582912 | tf_op jit(solution)/shard_map/pallas_call | solution.py:382
  155.5 14.6 %all-to-all-done = bf16[8,1,512,384]{3,2,1,0:T(8,128)(2,1)S(1)} async-done(((bf16[8,1,512,384]{3,2,1,0:T(8,128)(2,1)}), bf16[8,1,512,384]{3,2,1,0:T(8,128)(2,1)S(1)}, u32[]{:S(2)}, u32[]{:S(2)}) %all-to-all-start) | async-done | bytes 3145760 | tf_op jit(solution)/shard_map/all_to_all | solution.py:1288
  173.8 4.5 all-to-all-start.1
  178.3 43.8 %shard_map.367 = (bf16[1,2,4096,4096]{3,2,1,0:T(8,128)(2,1)}, bf16[1,4096,128]{2,1,0:T(8,128)(2,1)}, f32[1,4096,128]{2,1,0:T(8,128)}, f32[1,4096,128]{2,1,0:T(8,128)}) custom-call(bf16[1,4096,384]{2,1,0:T(8,128)(2,1)} %bitcast.166, bf16[1,4096,384]{2,1,0:T(8,128)(2,1)} %bitcast.167, bf16[1,4096,384]{2,1,0:T(8,128)(2,1)} %bitcast.168), custom_call_target="tpu_custom_call" | custom-call | flops 34359738368 | bytes 67108864 | tf_op jit(solution)/shard_map/pallas_call | solution.py:175
  222.0 6.2 all-to-all-done.1
  232.7 44.0 %shard_map.369 = (bf16[1,2,4096,4096]{3,2,1,0:T(8,128)(2,1)}, bf16[1,4096,128]{2,1,0:T(8,128)(2,1)}, f32[1,4096,128]{2,1,0:T(8,128)}, f32[1,4096,128]{2,1,0:T(8,128)}) custom-call(bf16[1,4096,384]{2,1,0:T(8,128)(2,1)} %bitcast.24.query_ref.key_ref.value_ref, bf16[1,4096,384]{2,1,0:T(8,128)(2,1)} %bitcast.24.query_ref.key_ref.value_ref, ...), custom_call_target="tpu_custom_call" | custom-call | flops 34359738368 | bytes 67108864 | tf_op jit(solution)/shard_map/pallas_call | solution.py:175
  276.7 8.5 all-to-all-done.3
  288.8 44.2 %shard_map.372 = (bf16[1,2,4096,4096]{3,2,1,0:T(8,128)(2,1)}, bf16[1,4096,128]{2,1,0:T(8,128)(2,1)}, f32[1,4096,128]{2,1,0:T(8,128)}, f32[1,4096,128]{2,1,0:T(8,128)}) custom-call(bf16[1,4096,384]{2,1,0:T(8,128)(2,1)} %bitcast.35.query_ref.key_ref.value_ref, bf16[1,4096,384]{2,1,0:T(8,128)(2,1)} %bitcast.35.query_ref.key_ref.value_ref, ...), custom_call_target="tpu_custom_call" | custom-call | flops 34359738368 | bytes 67108864 | tf_op jit(solution)/shard_map/pallas_call | solution.py:175
  333.0 5.9 all-gather.6.cloned.1.call-done
  343.2 40.6 %shard_map.371 = (bf16[512,1024]{1,0:T(8,128)(2,1)}, bf16[512,4096]{1,0:T(8,128)(2,1)}, bf16[512,1024]{1,0:T(8,128)(2,1)}, bf16[512,4096]{1,0:T(8,128)(2,1)}, bf...) custom-call(bf16[8,512,128]{2,1,0:T(8,128)(2,1)} %bitcast.178, ...), custom_call_target="tpu_custom_call" | custom-call | flops 19327352832 | bytes 34603008 | tf_op jit(solution)/shard_map/pallas_call | solution.py:627
  388.2 40.6 %shard_map.373 = (bf16[512,1024]{1,0:T(8,128)(2,1)}, bf16[512,4096]{1,0:T(8,128)(2,1)}, bf16[512,1024]{1,0:T(8,128)(2,1)}, bf16[512,4096]{1,0:T(8,128)(2,1)}, bf...) custom-call(bf16[8,512,128]{2,1,0:T(8,128)(2,1)} %bitcast.38.mixed_r, ...), custom_call_target="tpu_custom_call" | custom-call | flops 19327352832 | bytes 34603008 | tf_op jit(solution)/shard_map/pallas_call | solution.py:627
  434.0 41.0 %shard_map.374 = (bf16[512,1024]{1,0:T(8,128)(2,1)}, bf16[512,4096]{1,0:T(8,128)(2,1)}, bf16[512,1024]{1,0:T(8,128)(2,1)}, bf16[512,4096]{1,0:T(8,128)(2,1)}, bf...) custom-call(bf16[8,512,128]{2,1,0:T(8,128)(2,1)} %bitcast.183, ...), custom_call_target="tpu_custom_call" | custom-call | flops 19327352832 | bytes 34603008 | tf_op jit(solution)/shard_map/pallas_call | solution.py:627
  475.1 42.7 %shard_map.375 = bf16[4,1024,2304]{2,1,0:T(8,128)(2,1)} custom-call(bf16[512,1024]{1,0:T(8,128)(2,1)} %get-tuple-element.165.refs_0_, bf16[512,1024]{1,0:T(8,128)(2,1)} %get-tuple-element.166.refs_1_, bf16[512,1024]{1,0:T(8,128)(2,1)} %get-tuple-element.168.refs_2_, bf16[512,4096]{1,0:T(8,128)(2,1)} %get-tuple-element.169.refs_3_, ...), custom_call_target="tpu_custom_call" | custom-call | flops 28991029248 | bytes 56623104 | tf_op jit(solution)/shard_map/pallas_call | solution.py:796
  520.8 4.6 all-to-all-start.8
  525.4 70.2 %shard_map.376 = bf16[1,4096,384]{2,1,0:T(8,128)(2,1)} custom-call(bf16[1,2,4096,4096]{3,2,1,0:T(8,128)(2,1)} %get-tuple-element.161.exps_ref, bf16[1,4096,384]{2,1,0:T(8,128)(2,1)} %bitcast.169, bf16[1,4096,384]{2,1,0:T(8,128)(2,1)} %bitcast.170, bf16[1,4096,384]{2,1,0:T(8,128)(2,1)} %bitcast.171, bf16[1,4096,128]{2,1,0:T(8,128)(2,1)} %bitcast.180, ...), custom_call_target="tpu_custom_call" | custom-call | flops 68719476736 | bytes 67108864 | tf_op jit(solution)/shard_map/pallas_call | solution.py:294
  595.6 4.7 all-to-all-start.7
  603.5 69.6 %shard_map.377 = bf16[1,4096,384]{2,1,0:T(8,128)(2,1)} custom-call(bf16[1,2,4096,4096]{3,2,1,0:T(8,128)(2,1)} %get-tuple-element.184.exps_ref, bf16[1,4096,384]{2,1,0:T(8,128)(2,1)} %bitcast.24.query_ref.key_ref.value_ref, bf16[1,4096,384]{2,1,0:T(8,128)(2,1)} %bitcast.24.query_ref.key_ref.value_ref, ...), custom_call_target="tpu_custom_call" | custom-call | flops 68719476736 | bytes 67108864 | tf_op jit(solution)/shard_map/pallas_call | solution.py:294
  673.1 4.9 all-to-all-start.9
  678.0 70.1 %shard_map.378 = bf16[1,4096,384]{2,1,0:T(8,128)(2,1)} custom-call(bf16[1,2,4096,4096]{3,2,1,0:T(8,128)(2,1)} %get-tuple-element.191.exps_ref, bf16[1,4096,384]{2,1,0:T(8,128)(2,1)} %bitcast.35.query_ref.key_ref.value_ref, bf16[1,4096,384]{2,1,0:T(8,128)(2,1)} %bitcast.35.query_ref.key_ref.value_ref, ...), custom_call_target="tpu_custom_call" | custom-call | flops 68719476736 | bytes 67108864 | tf_op jit(solution)/shard_map/pallas_call | solution.py:294
  752.6 14.3 %shard_map.379 = (f32[2,8,1024]{2,1,0:T(8,128)}, f32[128,1024]{1,0:T(8,128)}) custom-call(bf16[8,512,384]{2,1,0:T(8,128)(2,1)} %bitcast.51.grad_ref.refs_3_, f32[512,1024]{1,0:T(8,128)} %get-tuple-element.141.rows_ref, f32[512,1024]{1,0:T(8,128)} %get-tuple-element.155.grad_rows_ref, f32[8,8192]{1,0:T(8,128)} %bitcast.195, ...), custom_call_target="tpu_custom_call" | custom-call | flops 3221225472 | bytes 14680064 | tf_op jit(solution)/shard_map/pallas_call | solution.py:728
  766.9 14.0 %shard_map.380 = (f32[2,8,1024]{2,1,0:T(8,128)}, f32[128,1024]{1,0:T(8,128)}) custom-call(bf16[8,512,384]{2,1,0:T(8,128)(2,1)} %bitcast.58.grad_ref.refs_4_, f32[512,1024]{1,0:T(8,128)} %get-tuple-element.145.rows_ref, f32[512,1024]{1,0:T(8,128)} %get-tuple-element.163.grad_rows_ref, f32[8,8192]{1,0:T(8,128)} %bitcast.192, ...), custom_call_target="tpu_custom_call" | custom-call | flops 3221225472 | bytes 14680064 | tf_op jit(solution)/shard_map/pallas_call | solution.py:728
  780.9 9.0 all-to-all-done.10
  789.9 17.9 %shard_map.381 = bf16[4,1024,768]{2,1,0:T(8,128)(2,1)} custom-call(bf16[512,1024]{1,0:T(8,128)(2,1)} %get-tuple-element.158.refs_0_, bf16[512,1024]{1,0:T(8,128)(2,1)} %get-tuple-element.159.refs_1_, bf16[512,1024]{1,0:T(8,128)(2,1)} %get-tuple-element.160.refs_2_, bf16[8,512,384]{2,1,0:T(8,128)(2,1)} %bitcast.51.grad_ref.refs_3_, ...), custom_call_target="tpu_custom_call" | custom-call | flops 9663676416 | bytes 18874368 | tf_op jit(solution)/shard_map/pallas_call | solution.py:796
  812.5 14.3 %shard_map.382 = (f32[2,8,1024]{2,1,0:T(8,128)}, f32[128,1024]{1,0:T(8,128)}) custom-call(bf16[8,512,384]{2,1,0:T(8,128)(2,1)} %bitcast.62.refs_5_.grad_ref, f32[512,1024]{1,0:T(8,128)} %get-tuple-element.146.rows_ref, f32[512,1024]{1,0:T(8,128)} %get-tuple-element.204.grad_rows_ref, f32[8,8192]{1,0:T(8,128)} %bitcast.189, ...), custom_call_target="tpu_custom_call" | custom-call | flops 3221225472 | bytes 14680064 | tf_op jit(solution)/shard_map/pallas_call | solution.py:728
  828.9 53.6 %shard_map.383 = (bf16[8,24,2048]{2,1,0:T(8,128)(2,1)S(1)}, f32[8,24,1024]{2,1,0:T(8,128)S(1)}, f32[32,128]{1,0:T(8,128)S(1)}) custom-call(f32[4,24,2048]{2,1,0:T(8,128)S(1)} %bitcast.148, f32[8,32,128]{2,1,0:T(8,128)S(1)} %bitcast_bitcast_fusion.patch_parts, bf16[1024,2048]{1,0:T(8,128)(2,1)} %all-gather.8.cloned.1.call-done.weight), custom_call_target="tpu_custom_call" | custom-call | tf_op jit(solution)/shard_map/pallas_call | solution.py:976
  897.4 35.7 %reduce-scatter.5.cloned.1.call-done.qkv_ref = bf16[128,768]{1,0:T(8,128)(2,1)} async-done(((bf16[4096,768]{1,0:T(8,128)(2,1)}), bf16[128,768]{1,0:T(8,128)(2,1)}) %reduce-scatter.5.cloned.1.call-update) | async-done | bytes 196624 | tf_op jit(solution)/shard_map/reduce_scatter | solution.py:1309
  936.8 9.9 %shard_map.384 = f32[8,128]{1,0:T(8,128)S(1)} custom-call(f32[8,128]{1,0:T(8,128)S(1)} %broadcast_in_dim.40.tile), custom_call_target="tpu_custom_call" | custom-call | tf_op jit(solution)/shard_map/pallas_call | solution.py:976
  948.6 9.7 %shard_map.385 = (f32[128,1792]{1,0:T(8,128)}, f32[1280,128]{1,0:T(8,128)}, f32[128,2048]{1,0:T(8,128)}, f32[160,1024]{1,0:T(8,128)}, f32[2,16,128]{2,1,0:T(8,12...) custom-call(f32[3]{0:T(128)} %pad_maximum_fusion.9.rates_ref, ...), custom_call_target="tpu_custom_call" | custom-call | tf_op jit(solution)/shard_map/pallas_call | solution.py:1381
  (174 shorter events, 86.8 us)
Async XLA Ops:
  7.2 9.0 copy-start.3
  7.2 9.9 %copy-start.30 = (f32[2,16,128]{2,1,0:T(8,128)S(1)}, f32[2,16,128]{2,1,0:T(8,128)}, u32[]{:S(2)}) copy-start(f32[2,16,128]{2,1,0:T(8,128)} %refs_4_.1) | copy-start | bytes 49156
  7.2 9.9 %copy-start.10 = (f32[160,1024]{1,0:T(8,128)S(1)}, f32[160,1024]{1,0:T(8,128)}, u32[]{:S(2)}) copy-start(f32[160,1024]{1,0:T(8,128)} %refs_3_.1) | copy-start | bytes 1966084
  7.2 10.0 %copy-start.5 = (f32[128,2048]{1,0:T(8,128)S(1)}, f32[128,2048]{1,0:T(8,128)}, u32[]{:S(2)}) copy-start(f32[128,2048]{1,0:T(8,128)} %refs_2_.1) | copy-start | bytes 3145732
  7.2 110.5 %all-gather.4.cloned.1.call-start = ((), (), s32[]{:S(2)}) async-start(), calls=%async_computation.13 | async-start | bytes 6488064 | tf_op jit(solution)/shard_map/all_gather | solution.py:1303
  11.3 54.7 %collective-permute-start = (bf16[2,3,8,8,128]{4,3,2,1,0:T(8,128)(2,1)}, bf16[2,3,8,8,128]{4,3,2,1,0:T(8,128)(2,1)}, u32[]{:S(2)}, u32[]{:S(2)}) collective-permute-start(bf16[2,3,8,8,128]{4,3,2,1,0:T(8,128)(2,1)} %pad_maximum_fusion.6), channel_id=1, source_target_pairs={{0,0},{1,8},{2,16},{3,24},{8,1},{9,9},{10,17},{11,25},{16,2},{17,1... | collective-permute-start | bytes 294920 | tf_op jit(solution)/shard_map/ppermute | solution.py:845
  17.3 48.3 %copy-start.4 = (bf16[128,2048]{1,0:T(8,128)(2,1)}, bf16[128,2048]{1,0:T(8,128)(2,1)S(1)}, u32[]{:S(2)}) copy-start(bf16[128,2048]{1,0:T(8,128)(2,1)S(1)} %convert_element_type.85) | copy-start | bytes 1572868
  129.1 41.0 %all-to-all-start = ((bf16[8,1,512,384]{3,2,1,0:T(8,128)(2,1)}), bf16[8,1,512,384]{3,2,1,0:T(8,128)(2,1)S(1)}, u32[]{:S(2)}, u32[]{:S(2)}) async-start(bf16[8,1,512,384]{3,2,1,0:T(8,128)(2,1)} %bitcast.177), calls=%async_computation | async-start | bytes 6291456 | tf_op jit(solution)/shard_map/all_to_all | solution.py:1288
  132.7 206.1 %all-gather.6.cloned.1.call-start = ((), (), s32[]{:S(2)}) async-start(), calls=%async_computation.14 | async-start | bytes 19464192 | tf_op jit(solution)/shard_map/all_gather | solution.py:1303
  144.1 26.0 %copy-start.29 = (bf16[1,16,8,128]{3,1,0,2:T(8,128)(2,1)S(1)}, bf16[1,16,8,128]{3,1,0,2:T(8,128)(2,1)}, u32[]{:S(2)}) copy-start(bf16[1,16,8,128]{3,1,0,2:T(8,128)(2,1)} %get-tuple-element.253) | copy-start | bytes 98308
  173.8 54.5 %all-to-all-start.1 = ((bf16[8,1,512,384]{3,2,1,0:T(8,128)(2,1)}), bf16[8,1,512,384]{3,2,1,0:T(8,128)(2,1)}, u32[]{:S(2)}, u32[]{:S(2)}) async-start(bf16[8,1,512,384]{3,2,1,0:T(8,128)(2,1)} %bitcast.173), calls=%async_computation.1 | async-start | bytes 6291456 | tf_op jit(solution)/shard_map/all_to_all | solution.py:1288
  228.3 56.9 %all-to-all-start.3 = ((bf16[8,1,512,384]{3,2,1,0:T(8,128)(2,1)}), bf16[8,1,512,384]{3,2,1,0:T(8,128)(2,1)}, u32[]{:S(2)}, u32[]{:S(2)}) async-start(bf16[8,1,512,384]{3,2,1,0:T(8,128)(2,1)} %bitcast.172), calls=%async_computation.3 | async-start | bytes 6291456 | tf_op jit(solution)/shard_map/all_to_all | solution.py:1288
  285.2 53.7 %all-to-all-start.2 = ((bf16[8,1,512,128]{3,2,1,0:T(8,128)(2,1)}), bf16[8,1,512,128]{3,2,1,0:T(8,128)(2,1)S(1)}, u32[]{:S(2)}, u32[]{:S(2)}) async-start(bf16[8,1,512,128]{3,2,1,0:T(8,128)(2,1)} %bitcast.186), calls=%async_computation.2 | async-start | bytes 2097152 | tf_op jit(solution)/shard_map/all_to_all | solution.py:1298
  288.7 229.1 %all-gather.8.cloned.1.call-start = ((), (), s32[]{:S(2)}) async-start(), calls=%async_computation.15 | async-start | bytes 4718592 | tf_op jit(solution)/shard_map/all_gather | solution.py:1499
  338.9 44.9 %all-to-all-start.4 = ((bf16[8,1,512,128]{3,2,1,0:T(8,128)(2,1)}), bf16[8,1,512,128]{3,2,1,0:T(8,128)(2,1)}, u32[]{:S(2)}, u32[]{:S(2)}) async-start(bf16[8,1,512,128]{3,2,1,0:T(8,128)(2,1)} %bitcast.185), calls=%async_computation.4 | async-start | bytes 2097152 | tf_op jit(solution)/shard_map/all_to_all | solution.py:1298
  383.8 45.0 %all-to-all-start.5 = ((bf16[8,1,512,128]{3,2,1,0:T(8,128)(2,1)}), bf16[8,1,512,128]{3,2,1,0:T(8,128)(2,1)S(1)}, u32[]{:S(2)}, u32[]{:S(2)}) async-start(bf16[8,1,512,128]{3,2,1,0:T(8,128)(2,1)} %bitcast.182), calls=%async_computation.5 | async-start | bytes 2097152 | tf_op jit(solution)/shard_map/all_to_all | solution.py:1298
  429.8 45.3 %all-to-all-start.6 = ((bf16[8,1,512,128]{3,2,1,0:T(8,128)(2,1)}), bf16[8,1,512,128]{3,2,1,0:T(8,128)(2,1)S(1)}, u32[]{:S(2)}, u32[]{:S(2)}) async-start(bf16[8,1,512,128]{3,2,1,0:T(8,128)(2,1)} %bitcast.181), calls=%async_computation.6 | async-start | bytes 2097152 | tf_op jit(solution)/shard_map/all_to_all | solution.py:1288
  434.0 355.9 %reduce-scatter.3.cloned.1.call-start = ((), (), s32[]{:S(2)}) async-start(), calls=%async_computation.16 | async-start | bytes 19464192 | tf_op jit(solution)/shard_map/reduce_scatter | solution.py:1309
  475.1 42.7 %copy-start.14 = (bf16[8,1,512,128]{3,2,1,0:T(8,128)(2,1)}, bf16[8,1,512,128]{3,2,1,0:T(8,128)(2,1)S(1)}, u32[]{:S(2)}) copy-start(bf16[8,1,512,128]{3,2,1,0:T(8,128)(2,1)S(1)} %all-to-all-done.6) | copy-start | bytes 3145732
  520.8 74.8 %all-to-all-start.8 = ((bf16[8,1,1024,128]{3,2,1,0:T(8,128)(2,1)}), bf16[8,1,1024,128]{3,2,1,0:T(8,128)(2,1)}, u32[]{:S(2)}, u32[]{:S(2)}) async-start(bf16[8,1,1024,128]{3,2,1,0:T(8,128)(2,1)} %bitcast.53), calls=%async_computation.8 | async-start | bytes 4194304 | tf_op jit(solution)/shard_map/all_to_all | solution.py:1288
  595.6 77.5 %all-to-all-start.7 = ((bf16[8,1,512,384]{3,2,1,0:T(8,128)(2,1)}), bf16[8,1,512,384]{3,2,1,0:T(8,128)(2,1)}, u32[]{:S(2)}, u32[]{:S(2)}) async-start(bf16[8,1,512,384]{3,2,1,0:T(8,128)(2,1)} %bitcast.175), calls=%async_computation.7 | async-start | bytes 6291456 | tf_op jit(solution)/shard_map/all_to_all | solution.py:1298
  673.1 75.0 %all-to-all-start.9 = ((bf16[8,1,512,384]{3,2,1,0:T(8,128)(2,1)}), bf16[8,1,512,384]{3,2,1,0:T(8,128)(2,1)}, u32[]{:S(2)}, u32[]{:S(2)}) async-start(bf16[8,1,512,384]{3,2,1,0:T(8,128)(2,1)} %bitcast.176), calls=%async_computation.9 | async-start | bytes 6291456 | tf_op jit(solution)/shard_map/all_to_all | solution.py:1298
  748.1 41.8 %all-to-all-start.10 = ((bf16[8,1,512,384]{3,2,1,0:T(8,128)(2,1)}), bf16[8,1,512,384]{3,2,1,0:T(8,128)(2,1)}, u32[]{:S(2)}, u32[]{:S(2)}) async-start(bf16[8,1,512,384]{3,2,1,0:T(8,128)(2,1)} %bitcast.174), calls=%async_computation.10 | async-start | bytes 6291456 | tf_op jit(solution)/shard_map/all_to_all | solution.py:1298
  752.6 180.6 %reduce-scatter.5.cloned.1.call-start = ((), (), s32[]{:S(2)}) async-start(), calls=%async_computation.17 | async-start | bytes 6488064 | tf_op jit(solution)/shard_map/reduce_scatter | solution.py:1309
  807.8 4.7 copy-start.26
  807.8 4.7 copy-start.31
  807.8 4.7 copy-start.28
  807.8 4.7 copy-start.32
  812.5 15.4 %copy-start.27 = (f32[6,8,1024]{2,1,0:T(8,128)S(1)}, f32[6,8,1024]{2,1,0:T(8,128)}, u32[]{:S(2)}) copy-start(f32[6,8,1024]{2,1,0:T(8,128)} %get-tuple-element.206) | copy-start | bytes 589828
  828.9 54.3 %copy-start.19 = (f32[192,1024]{1,0:T(8,128)S(1)}, f32[192,1024]{1,0:T(8,128)}, u32[]{:S(2)}) copy-start(f32[192,1024]{1,0:T(8,128)} %copy-done.18) | copy-start | bytes 2359300
  828.9 55.3 %copy-start.9 = (f32[192,1024]{1,0:T(8,128)S(1)}, f32[192,1024]{1,0:T(8,128)}, u32[]{:S(2)}) copy-start(f32[192,1024]{1,0:T(8,128)} %copy-done.8) | copy-start | bytes 2359300
  890.5 5.0 copy-start.21
  (21 other events, 46.9 us)
Sparse Core Ops, SparseCore 0:
  11.5 78.6 all-gather.3
  170.2 168.5 all-gather.5
  341.3 40.5 all-gather.7
  518.0 243.7 reduce-scatter.2
  808.0 125.1 reduce-scatter.4
where the time goes:
time: 975 us; the launch traced here: 966 us
  Pallas kernels  760 us (78%)
  waiting for transfers between devices  79.9 us (8%)
  starting transfers between devices  49.9 us (5%)
  between operations  23.4 us (2%)
  local copies, waits for them, and re-layouts  22.5 us (2%)
  other arithmetic  20.8 us (2%)
    pallas_call x3, Pallas kernels, attend_back(): pl.pallas_call(partial(attend_back_kernel, chunk), grid=(units, query_tot...  210 us
    pallas_call x4, Pallas kernels, remote_call(): pl.pallas_call(kernel, out_shape=out_shape, in_specs=[in_vmem] * len(oper...  147 us
    pallas_call x3, Pallas kernels, attend(): pl.pallas_call(partial(attend_kernel, chunk), grid=(units, query_total //...  132 us
    pallas_call x3, Pallas kernels, middle_layer(): pl.pallas_call(partial(middle_kernel, head_cols, hidden_cols), in_specs=[...  122 us
    pallas_call x2, Pallas kernels, weight_grads(): pl.pallas_call(partial(weight_kernel, clips, len(terms)), grid=(blocks,),...  60.6 us
    pallas_call x3, Pallas kernels, close_layer(): pl.pallas_call(partial(close_kernel, blocks), grid=(blocks,), in_specs=[p...  42.6 us
    reduce_scatter x2, waiting for transfers between devices, scatter_blocks(): return lax.psum_scatter(flat, EVERY, scatter_dimension=0, tiled=True)  35.7 us
    pallas_call x3, Pallas kernels, open_layer(): pl.pallas_call(open_kernel, grid=(blocks,), in_specs=[pl.BlockSpec(patch_...  34 us
  transfers between devices with their start and end apart: 17, of which 6 were waited for; matrix products, arithmetic and copies ran while one was open for 5% of the time, Pallas kernels for 73%

commit v1 on v0

--- a/solution.py
+++ b/solution.py
@@ -363,7 +363,7 @@
             )
             return unused
 
-        lax.fori_loop(0, groups, one_group, 0)
+        lax.fori_loop(0, groups, one_group, 0, unroll=True)
 
     columns = send_ref.shape[2]
     for place in range(send_ref.shape[0]):
@@ -498,7 +498,7 @@
             one_group(group, group_rows(group, rows_group))
             return unused
 
-        lax.fori_loop(0, groups, step, 0)
+        lax.fori_loop(0, groups, step, 0, unroll=True)
 
     each_block(lambda block: fetch_out(block).start())
     each_block(lambda block: fetch_wide(block).start())
@@ -713,7 +713,7 @@
             grad_embed_ref[...] += contract(patch_ref[rows, :], grad_low, 0, 0)
             return unused
 
-        lax.fori_loop(0, groups, one_group, 0)
+        lax.fori_loop(0, groups, one_group, 0, unroll=True)
 
 
 def close_layer(grad_pairs, rows_in, grad_rows, mods, patch_rows, w_qkv):
@@ -1129,9 +1129,9 @@
     patch_received[here] = patch_parts[here]
     for copy in copies:
         copy.wait()
-    total = mod_received[0]
+    total = mod_received[0].astype(jnp.float32)
     for place in range(1, dp_size):
-        total = total + mod_received[place]
+        total = total + mod_received[place].astype(jnp.float32)
     mod_block[...] = to_half(total)
     total = patch_received[0]
     for place in range(1, plane):
@@ -1152,7 +1152,7 @@
     mod_copies = plane_copies(
         lambda other: mod_swapped, lambda own: mod_all.at[own], spread_send, spread_receive
     )
-    cond_part[...] = contract(mod_swapped[...], weight[...], 1, 1)
+    cond_part[...] = to_half(contract(mod_swapped[...], weight[...], 1, 1))
     cond_copies = axis_copies(
         "tensor",
         lambda other: cond_part,
@@ -1166,19 +1166,19 @@
     cond_tensor[column] = cond_part[...]
     for copy in patch_copies + cond_copies:
         copy.wait()
-    total = cond_tensor[0]
+    total = cond_tensor[0].astype(jnp.float32)
     total_patch = patch_tensor[0]
     for place in range(1, tensor_size):
-        total = total + cond_tensor[place]
+        total = total + cond_tensor[place].astype(jnp.float32)
         total_patch = total_patch + patch_tensor[place]
     patch_out[...] = total_patch
-    cond_block[...] = total
+    cond_block[...] = to_half(total)
     gather_copies = plane_copies(
         lambda other: cond_block, lambda own: cond_all.at[own], gather_send, gather_receive
     )
     for copy in gather_copies:
         copy.start()
-    cond_all[here] = total
+    cond_all[here] = cond_block[...]
     for copy in gather_copies + mod_copies:
         copy.wait()
 
@@ -1191,6 +1191,9 @@
 
     def held(*shape):
         return pltpu.VMEM(shape, jnp.float32)
+
+    def low(*shape):
+        return pltpu.VMEM(shape, jnp.bfloat16)
 
     def sems(*counts):
         return [pltpu.SemaphoreType.DMA((count,)) for count in counts]
@@ -1201,19 +1204,19 @@
         2,
         [
             jax.ShapeDtypeStruct((plane, rows, columns), jnp.bfloat16),
-            jax.ShapeDtypeStruct((plane, rows, features), jnp.float32),
+            jax.ShapeDtypeStruct((plane, rows, features), jnp.bfloat16),
             jax.ShapeDtypeStruct(patch_shape, jnp.float32),
         ],
         [
-            held(*mod_parts.shape),
+            low(*mod_parts.shape),
             held(*patch_parts.shape),
-            pltpu.VMEM((rows, columns), jnp.bfloat16),
+            low(rows, columns),
             held(*patch_shape),
             held(tensor_size, *patch_shape),
-            held(rows, features),
-            held(tensor_size, rows, features),
-            pltpu.VMEM((rows, columns), jnp.bfloat16),
-            held(rows, features),
+            low(rows, features),
+            low(tensor_size, rows, features),
+            low(rows, columns),
+            low(rows, features),
         ]
         + sems(1, 1, dp_size - 1, dp_size - 1, *[plane - 1] * 4)
         + sems(*[tensor_size - 1] * 4, plane - 1, plane - 1),
@@ -1307,6 +1310,47 @@
 def scatter_blocks(blocks_in):
     flat = blocks_in.reshape(-1, blocks_in.shape[-1])
     return lax.psum_scatter(flat, EVERY, scatter_dimension=0, tiled=True)
+
+
+def scatter_stages(blocks_in):
+    dp_size, frame_size, tensor_size, row, frame, column = places()
+    pairs_dp = dp_size // 2
+    side = lax.rem(row, 2)
+    columns = blocks_in.shape[-1]
+    parted = blocks_in.reshape(tensor_size, pairs_dp, 2, frame_size, -1, columns)
+
+    def of_side(which):
+        return lax.dynamic_index_in_dim(parted, which, 2, keepdims=False)
+
+    swaps = [(place, place + 1 - 2 * (place % 2)) for place in range(dp_size)]
+    received = lax.ppermute(of_side(1 - side), "dp", swaps)
+    halves = to_half(of_side(side).astype(jnp.float32) + received.astype(jnp.float32))
+    members = pairs_dp * frame_size
+    halves = jnp.moveaxis(halves, 0, 2).reshape(members, tensor_size, -1, columns)
+    here = lax.div(row, 2) * frame_size + frame
+    total = lax.dynamic_index_in_dim(halves, here, 0, keepdims=False).astype(jnp.float32)
+    moved = []
+    for shift in range(1, members):
+        routes = []
+        for source in range(members):
+            target = (source + shift) % members
+            for core in range(2):
+                source_row = source // frame_size * 2 + core
+                target_row = target // frame_size * 2 + core
+                routes.append(
+                    (
+                        source_row * frame_size + source % frame_size,
+                        target_row * frame_size + target % frame_size,
+                    )
+                )
+        block = lax.dynamic_index_in_dim(
+            halves, lax.rem(here + shift, members), 0, keepdims=False
+        )
+        moved.append(lax.ppermute(block, PLANE, routes))
+    for block in moved:
+        total = total + block.astype(jnp.float32)
+    over_tensor = lax.all_to_all(to_half(total), "tensor", 0, 0, tiled=True)
+    return jnp.sum(over_tensor.astype(jnp.float32), axis=0)
 
 
 def pad_lanes(rows_in, axis):
@@ -1568,7 +1612,7 @@
                 grad_pairs[clip], scattered_rest, *[parts[0] for parts in closed]
             )
             grad_wqkv = weight_grads(blocks, [(flat_one, grad_pairs)])
-            scattered_qkv = scatter_blocks(grad_wqkv)
+            scattered_qkv = scatter_stages(grad_wqkv)
             grad_pairs[clip] = after(grad_pairs[clip], grad_wqkv)
         closed.append(
             close_layer(
@@ -1586,9 +1630,9 @@
     mod_parts = jnp.transpose(
         grad_mod.reshape(clips, dp_size, -1, frames_here, D), (1, 0, 3, 2, 4)
     ).reshape(dp_size, groups, -1)
-    mod_all, cond_places, patch_block = cond_sums(mod_parts, patch_parts, cond_whole)
+    mod_all, cond_places, patch_block = cond_sums(to_half(mod_parts), patch_parts, cond_whole)
     mod_all = mod_all.reshape(-1, mod_all.shape[-1])
-    grad_cond_all = cond_places.reshape(-1, D)
+    grad_cond_all = cond_places.reshape(-1, D).astype(jnp.float32)
     final_patch = patch_block.reshape(2, PD, patch_cols)
     final_cond = rows_product(cond_own, mod_all)
     unused, silu_cond = jax.vjp(jax.nn.silu, cond_vec)

time: 975 us -> 949 us (0.973)
  waiting for transfers between devices: 79.9 us -> 49.3 us
  Pallas kernels: 760 us -> 744 us
    reduce_scatter x2 -> x1, waiting for transfers between devices: 35.7 us -> 0.01 us  [scatter_blocks(): return lax.psum_scatter(flat, EVERY, scatter_dimension=0, tiled=True)]
    pallas_call x3, Pallas kernels: 122 us -> 106 us  [middle_layer(): pl.pallas_call(partial(middle_kernel, head_cols, hidden_cols), in_specs=[...]
  transfers between devices with their start and end apart: 17 -> 21, of which waited for: 6 -> 5; matrix products, arithmetic and copies ran while one was open for 5% -> 5% of each run, Pallas kernels for 73% -> 74%
where the time goes in v1:
time: 949 us; the launch traced here: 940 us
  Pallas kernels  744 us (78%)
  starting transfers between devices  58.8 us (6%)
  waiting for transfers between devices  49.3 us (5%)
  other arithmetic  29.7 us (3%)
  local copies, waits for them, and re-layouts  24.1 us (3%)
  between operations  23.3 us (2%)
  matrix products  10.8 us (1%)
    pallas_call x3, Pallas kernels, attend_back(): pl.pallas_call(partial(attend_back_kernel, chunk), grid=(units, query_tot...  210 us
    pallas_call x4, Pallas kernels, remote_call(): pl.pallas_call(kernel, out_shape=out_shape, in_specs=[in_vmem] * len(oper...  152 us
    pallas_call x3, Pallas kernels, attend(): pl.pallas_call(partial(attend_kernel, chunk), grid=(units, query_total //...  140 us
    pallas_call x3, Pallas kernels, middle_layer(): pl.pallas_call(partial(middle_kernel, head_cols, hidden_cols), in_specs=[...  106 us
    pallas_call x2, Pallas kernels, weight_grads(): pl.pallas_call(partial(weight_kernel, clips, len(terms)), grid=(blocks,),...  60.7 us
    pallas_call x3, Pallas kernels, close_layer(): pl.pallas_call(partial(close_kernel, blocks), grid=(blocks,), in_specs=[p...  36 us
    pallas_call x3, Pallas kernels, open_layer(): pl.pallas_call(open_kernel, grid=(blocks,), in_specs=[pl.BlockSpec(patch_...  26.9 us
    all_to_all x6, starting transfers between devices, to_tokens(): moved = lax.all_to_all(by_place, axes, 0, 0, tiled=True)  26.8 us
  transfers between devices with their start and end apart: 21, of which 5 were waited for; matrix products, arithmetic and copies ran while one was open for 5% of the time, Pallas kernels for 74%

profile of v1, /device:TPU:0, one launch (start us, length us, event | category | flops | bytes accessed | tf_op | source)
XLA Modules:
  0.0 940.3 jit_solution(4693406686301371293)
XLA Ops:
  17.3 44.9 %shard_map.363 = (bf16[8,160,1024]{2,1,0:T(8,128)(2,1)S(1)}, bf16[8,2,16,128]{3,2,1,0:T(8,128)(2,1)S(1)}, f32[8,8,128]{2,1,0:T(8,128)S(1)}) custom-call(bf16[160,1024]{1,0:T(8,128)(2,1)S(1)} %convert_element_type.121.refs_0_, bf16[2,16,128]{2,1,0:T(8,128)(2,1)S(1)} %convert_element_type.122.refs_1_, f32[8,128]{1,0:T(8,128)S(1)} %pad.19.refs_2_), custom_call_target="tpu_custom_call" | custom-call | tf_op jit(solution)/shard_map/pallas_call | solution.py:976
  77.9 38.2 %shard_map.364 = f32[4,24,2048]{2,1,0:T(8,128)S(1)} custom-call(f32[8,24,2048]{2,1,0:T(8,128)S(1)} %bitcast.160), custom_call_target="tpu_custom_call" | custom-call | tf_op jit(solution)/shard_map/pallas_call | solution.py:976
  117.8 8.9 shard_map.366
  130.7 9.0 shard_map.368
  139.7 9.0 shard_map.370
  148.6 19.1 %all-to-all-done = bf16[8,1,512,384]{3,2,1,0:T(8,128)(2,1)S(1)} async-done(((bf16[8,1,512,384]{3,2,1,0:T(8,128)(2,1)}), bf16[8,1,512,384]{3,2,1,0:T(8,128)(2,1)S(1)}, u32[]{:S(2)}, u32[]{:S(2)}) %all-to-all-start) | async-done | bytes 3145760 | tf_op jit(solution)/shard_map/all_to_all | solution.py:1291
  171.4 4.4 all-to-all-start.1
  175.9 43.7 %shard_map.367 = (bf16[1,2,4096,4096]{3,2,1,0:T(8,128)(2,1)}, bf16[1,4096,128]{2,1,0:T(8,128)(2,1)}, f32[1,4096,128]{2,1,0:T(8,128)}, f32[1,4096,128]{2,1,0:T(8,128)}) custom-call(bf16[1,4096,384]{2,1,0:T(8,128)(2,1)} %bitcast.182, bf16[1,4096,384]{2,1,0:T(8,128)(2,1)} %bitcast.183, bf16[1,4096,384]{2,1,0:T(8,128)(2,1)} %bitcast.184), custom_call_target="tpu_custom_call" | custom-call | flops 34359738368 | bytes 67108864 | tf_op jit(solution)/shard_map/pallas_call | solution.py:175
  219.5 6.4 all-to-all-done.1
  230.4 52.4 %shard_map.369 = (bf16[1,2,4096,4096]{3,2,1,0:T(8,128)(2,1)}, bf16[1,4096,128]{2,1,0:T(8,128)(2,1)}, f32[1,4096,128]{2,1,0:T(8,128)}, f32[1,4096,128]{2,1,0:T(8,128)}) custom-call(bf16[1,4096,384]{2,1,0:T(8,128)(2,1)} %bitcast.24.query_ref.key_ref.value_ref, bf16[1,4096,384]{2,1,0:T(8,128)(2,1)} %bitcast.24.query_ref.key_ref.value_ref, ...), custom_call_target="tpu_custom_call" | custom-call | flops 34359738368 | bytes 67108864 | tf_op jit(solution)/shard_map/pallas_call | solution.py:175
  286.9 44.5 %shard_map.372 = (bf16[1,2,4096,4096]{3,2,1,0:T(8,128)(2,1)}, bf16[1,4096,128]{2,1,0:T(8,128)(2,1)}, f32[1,4096,128]{2,1,0:T(8,128)}, f32[1,4096,128]{2,1,0:T(8,128)}) custom-call(bf16[1,4096,384]{2,1,0:T(8,128)(2,1)} %bitcast.35.query_ref.key_ref.value_ref, bf16[1,4096,384]{2,1,0:T(8,128)(2,1)} %bitcast.35.query_ref.key_ref.value_ref, ...), custom_call_target="tpu_custom_call" | custom-call | flops 34359738368 | bytes 67108864 | tf_op jit(solution)/shard_map/pallas_call | solution.py:175
  331.4 4.6 all-gather.6.cloned.1.call-done
  340.3 35.2 %shard_map.371 = (bf16[512,1024]{1,0:T(8,128)(2,1)}, bf16[512,4096]{1,0:T(8,128)(2,1)}, bf16[512,1024]{1,0:T(8,128)(2,1)}, bf16[512,4096]{1,0:T(8,128)(2,1)}, bf...) custom-call(bf16[8,512,128]{2,1,0:T(8,128)(2,1)} %bitcast.194, ...), custom_call_target="tpu_custom_call" | custom-call | flops 19327352832 | bytes 34603008 | tf_op jit(solution)/shard_map/pallas_call | solution.py:627
  379.8 35.2 %shard_map.373 = (bf16[512,1024]{1,0:T(8,128)(2,1)}, bf16[512,4096]{1,0:T(8,128)(2,1)}, bf16[512,1024]{1,0:T(8,128)(2,1)}, bf16[512,4096]{1,0:T(8,128)(2,1)}, bf...) custom-call(bf16[8,512,128]{2,1,0:T(8,128)(2,1)} %bitcast.38.mixed_r, ...), custom_call_target="tpu_custom_call" | custom-call | flops 19327352832 | bytes 34603008 | tf_op jit(solution)/shard_map/pallas_call | solution.py:627
  420.2 35.4 %shard_map.374 = (bf16[512,1024]{1,0:T(8,128)(2,1)}, bf16[512,4096]{1,0:T(8,128)(2,1)}, bf16[512,1024]{1,0:T(8,128)(2,1)}, bf16[512,4096]{1,0:T(8,128)(2,1)}, bf...) custom-call(bf16[8,512,128]{2,1,0:T(8,128)(2,1)} %bitcast.199, ...), custom_call_target="tpu_custom_call" | custom-call | flops 19327352832 | bytes 34603008 | tf_op jit(solution)/shard_map/pallas_call | solution.py:627
  455.6 42.8 %shard_map.375 = bf16[4,1024,2304]{2,1,0:T(8,128)(2,1)} custom-call(bf16[512,1024]{1,0:T(8,128)(2,1)} %get-tuple-element.165.refs_0_, bf16[512,1024]{1,0:T(8,128)(2,1)} %get-tuple-element.166.refs_1_, bf16[512,1024]{1,0:T(8,128)(2,1)} %get-tuple-element.168.refs_2_, bf16[512,4096]{1,0:T(8,128)(2,1)} %get-tuple-element.169.refs_3_, ...), custom_call_target="tpu_custom_call" | custom-call | flops 28991029248 | bytes 56623104 | tf_op jit(solution)/shard_map/pallas_call | solution.py:796
  501.5 4.5 all-to-all-start.8
  506.1 70.2 %shard_map.376 = bf16[1,4096,384]{2,1,0:T(8,128)(2,1)} custom-call(bf16[1,2,4096,4096]{3,2,1,0:T(8,128)(2,1)} %get-tuple-element.161.exps_ref, bf16[1,4096,384]{2,1,0:T(8,128)(2,1)} %bitcast.185, bf16[1,4096,384]{2,1,0:T(8,128)(2,1)} %bitcast.186, bf16[1,4096,384]{2,1,0:T(8,128)(2,1)} %bitcast.187, bf16[1,4096,128]{2,1,0:T(8,128)(2,1)} %bitcast.196, ...), custom_call_target="tpu_custom_call" | custom-call | flops 68719476736 | bytes 67108864 | tf_op jit(solution)/shard_map/pallas_call | solution.py:294
  576.2 4.7 all-to-all-start.7
  584.1 69.6 %shard_map.377 = bf16[1,4096,384]{2,1,0:T(8,128)(2,1)} custom-call(bf16[1,2,4096,4096]{3,2,1,0:T(8,128)(2,1)} %get-tuple-element.184.exps_ref, bf16[1,4096,384]{2,1,0:T(8,128)(2,1)} %bitcast.24.query_ref.key_ref.value_ref, bf16[1,4096,384]{2,1,0:T(8,128)(2,1)} %bitcast.24.query_ref.key_ref.value_ref, ...), custom_call_target="tpu_custom_call" | custom-call | flops 68719476736 | bytes 67108864 | tf_op jit(solution)/shard_map/pallas_call | solution.py:294
  653.7 4.9 all-to-all-start.9
  658.6 70.1 %shard_map.378 = bf16[1,4096,384]{2,1,0:T(8,128)(2,1)} custom-call(bf16[1,2,4096,4096]{3,2,1,0:T(8,128)(2,1)} %get-tuple-element.191.exps_ref, bf16[1,4096,384]{2,1,0:T(8,128)(2,1)} %bitcast.35.query_ref.key_ref.value_ref, bf16[1,4096,384]{2,1,0:T(8,128)(2,1)} %bitcast.35.query_ref.key_ref.value_ref, ...), custom_call_target="tpu_custom_call" | custom-call | flops 68719476736 | bytes 67108864 | tf_op jit(solution)/shard_map/pallas_call | solution.py:294
  728.6 4.6 all-to-all-start.10
  733.3 12.0 %shard_map.379 = (f32[2,8,1024]{2,1,0:T(8,128)}, f32[128,1024]{1,0:T(8,128)}) custom-call(bf16[8,512,384]{2,1,0:T(8,128)(2,1)} %bitcast.51.grad_ref.refs_3_, f32[512,1024]{1,0:T(8,128)} %get-tuple-element.141.rows_ref, f32[512,1024]{1,0:T(8,128)} %get-tuple-element.155.grad_rows_ref, f32[8,8192]{1,0:T(8,128)} %bitcast.211, ...), custom_call_target="tpu_custom_call" | custom-call | flops 3221225472 | bytes 14680064 | tf_op jit(solution)/shard_map/pallas_call | solution.py:728
  745.2 11.9 %shard_map.380 = (f32[2,8,1024]{2,1,0:T(8,128)}, f32[128,1024]{1,0:T(8,128)}) custom-call(bf16[8,512,384]{2,1,0:T(8,128)(2,1)} %bitcast.58.grad_ref.refs_4_, f32[512,1024]{1,0:T(8,128)} %get-tuple-element.145.rows_ref, f32[512,1024]{1,0:T(8,128)} %get-tuple-element.163.grad_rows_ref, f32[8,8192]{1,0:T(8,128)} %bitcast.208, ...), custom_call_target="tpu_custom_call" | custom-call | flops 3221225472 | bytes 14680064 | tf_op jit(solution)/shard_map/pallas_call | solution.py:728
  757.1 13.3 %all-to-all-done.10 = bf16[8,1,512,384]{3,2,1,0:T(8,128)(2,1)} async-done(((bf16[8,1,512,384]{3,2,1,0:T(8,128)(2,1)}), bf16[8,1,512,384]{3,2,1,0:T(8,128)(2,1)}, u32[]{:S(2)}, u32[]{:S(2)}) %all-to-all-start.10) | async-done | bytes 3145760 | tf_op jit(solution)/shard_map/all_to_all | solution.py:1301
  770.5 17.9 %shard_map.381 = bf16[4,1024,768]{2,1,0:T(8,128)(2,1)} custom-call(bf16[512,1024]{1,0:T(8,128)(2,1)} %get-tuple-element.158.refs_0_, bf16[512,1024]{1,0:T(8,128)(2,1)} %get-tuple-element.159.refs_1_, bf16[512,1024]{1,0:T(8,128)(2,1)} %get-tuple-element.160.refs_2_, bf16[8,512,384]{2,1,0:T(8,128)(2,1)} %bitcast.51.grad_ref.refs_3_, ...), custom_call_target="tpu_custom_call" | custom-call | flops 9663676416 | bytes 18874368 | tf_op jit(solution)/shard_map/pallas_call | solution.py:796
  798.1 12.1 %shard_map.382 = (f32[2,8,1024]{2,1,0:T(8,128)}, f32[128,1024]{1,0:T(8,128)}) custom-call(bf16[8,512,384]{2,1,0:T(8,128)(2,1)} %bitcast.62.refs_5_.grad_ref, f32[512,1024]{1,0:T(8,128)} %get-tuple-element.146.rows_ref, f32[512,1024]{1,0:T(8,128)} %get-tuple-element.204.grad_rows_ref, f32[8,8192]{1,0:T(8,128)} %bitcast.205, ...), custom_call_target="tpu_custom_call" | custom-call | flops 3221225472 | bytes 14680064 | tf_op jit(solution)/shard_map/pallas_call | solution.py:728
  820.1 60.2 %shard_map.383 = (bf16[8,24,2048]{2,1,0:T(8,128)(2,1)S(1)}, bf16[8,24,1024]{2,1,0:T(8,128)(2,1)S(1)}, f32[32,128]{1,0:T(8,128)S(1)}) custom-call(bf16[4,24,2048]{2,1,0:T(8,128)(2,1)S(1)} %bitcast.162, f32[8,32,128]{2,1,0:T(8,128)S(1)} %bitcast_bitcast_fusion.patch_parts, bf16[1024,2048]{1,0:T(8,128)(2,1)S(1)} %copy-done), custom_call_target="tpu_custom_call" | custom-call | tf_op jit(solution)/shard_map/pallas_call | solution.py:976
  902.0 5.8 all-to-all-done.11
  911.8 8.9 shard_map.384
  922.7 9.7 %shard_map.385 = (f32[128,1792]{1,0:T(8,128)}, f32[1280,128]{1,0:T(8,128)}, f32[128,2048]{1,0:T(8,128)}, f32[160,1024]{1,0:T(8,128)}, f32[2,16,128]{2,1,0:T(8,12...) custom-call(f32[3]{0:T(128)} %pad_maximum_fusion.9.rates_ref, ...), custom_call_target="tpu_custom_call" | custom-call | tf_op jit(solution)/shard_map/pallas_call | solution.py:1425
  (186 shorter events, 102.9 us)
Async XLA Ops:
  7.2 9.0 copy-start.4
  7.2 9.9 %copy-start.28 = (f32[2,16,128]{2,1,0:T(8,128)S(1)}, f32[2,16,128]{2,1,0:T(8,128)}, u32[]{:S(2)}) copy-start(f32[2,16,128]{2,1,0:T(8,128)} %refs_4_.1) | copy-start | bytes 49156
  7.2 9.9 %copy-start.11 = (f32[160,1024]{1,0:T(8,128)S(1)}, f32[160,1024]{1,0:T(8,128)}, u32[]{:S(2)}) copy-start(f32[160,1024]{1,0:T(8,128)} %refs_3_.1) | copy-start | bytes 1966084
  7.2 9.9 %copy-start.6 = (f32[128,2048]{1,0:T(8,128)S(1)}, f32[128,2048]{1,0:T(8,128)}, u32[]{:S(2)}) copy-start(f32[128,2048]{1,0:T(8,128)} %refs_2_.1) | copy-start | bytes 3145732
  7.2 110.6 %all-gather.4.cloned.1.call-start = ((), (), s32[]{:S(2)}) async-start(), calls=%async_computation.13 | async-start | bytes 6488064 | tf_op jit(solution)/shard_map/all_gather | solution.py:1306
  11.3 54.7 %collective-permute-start = (bf16[2,3,8,8,128]{4,3,2,1,0:T(8,128)(2,1)}, bf16[2,3,8,8,128]{4,3,2,1,0:T(8,128)(2,1)}, u32[]{:S(2)}, u32[]{:S(2)}) collective-permute-start(bf16[2,3,8,8,128]{4,3,2,1,0:T(8,128)(2,1)} %pad_maximum_fusion.6), channel_id=1, source_target_pairs={{0,0},{1,8},{2,16},{3,24},{8,1},{9,9},{10,17},{11,25},{16,2},{17,1... | collective-permute-start | bytes 294920 | tf_op jit(solution)/shard_map/ppermute | solution.py:845
  17.2 48.3 %copy-start.5 = (bf16[128,2048]{1,0:T(8,128)(2,1)}, bf16[128,2048]{1,0:T(8,128)(2,1)S(1)}, u32[]{:S(2)}) copy-start(bf16[128,2048]{1,0:T(8,128)(2,1)S(1)} %convert_element_type.126) | copy-start | bytes 1572868
  126.7 41.0 %all-to-all-start = ((bf16[8,1,512,384]{3,2,1,0:T(8,128)(2,1)}), bf16[8,1,512,384]{3,2,1,0:T(8,128)(2,1)S(1)}, u32[]{:S(2)}, u32[]{:S(2)}) async-start(bf16[8,1,512,384]{3,2,1,0:T(8,128)(2,1)} %bitcast.193), calls=%async_computation | async-start | bytes 6291456 | tf_op jit(solution)/shard_map/all_to_all | solution.py:1291
  130.4 205.6 %all-gather.6.cloned.1.call-start = ((), (), s32[]{:S(2)}) async-start(), calls=%async_computation.14 | async-start | bytes 19464192 | tf_op jit(solution)/shard_map/all_gather | solution.py:1306
  139.6 28.1 %copy-start.27 = (bf16[1,16,8,128]{3,1,0,2:T(8,128)(2,1)S(1)}, bf16[1,16,8,128]{3,1,0,2:T(8,128)(2,1)}, u32[]{:S(2)}) copy-start(bf16[1,16,8,128]{3,1,0,2:T(8,128)(2,1)} %get-tuple-element.256) | copy-start | bytes 98308
  171.4 54.5 %all-to-all-start.1 = ((bf16[8,1,512,384]{3,2,1,0:T(8,128)(2,1)}), bf16[8,1,512,384]{3,2,1,0:T(8,128)(2,1)}, u32[]{:S(2)}, u32[]{:S(2)}) async-start(bf16[8,1,512,384]{3,2,1,0:T(8,128)(2,1)} %bitcast.189), calls=%async_computation.1 | async-start | bytes 6291456 | tf_op jit(solution)/shard_map/all_to_all | solution.py:1291
  225.9 56.8 %all-to-all-start.3 = ((bf16[8,1,512,384]{3,2,1,0:T(8,128)(2,1)}), bf16[8,1,512,384]{3,2,1,0:T(8,128)(2,1)}, u32[]{:S(2)}, u32[]{:S(2)}) async-start(bf16[8,1,512,384]{3,2,1,0:T(8,128)(2,1)} %bitcast.188), calls=%async_computation.3 | async-start | bytes 6291456 | tf_op jit(solution)/shard_map/all_to_all | solution.py:1291
  282.8 53.2 %all-to-all-start.2 = ((bf16[8,1,512,128]{3,2,1,0:T(8,128)(2,1)}), bf16[8,1,512,128]{3,2,1,0:T(8,128)(2,1)S(1)}, u32[]{:S(2)}, u32[]{:S(2)}) async-start(bf16[8,1,512,128]{3,2,1,0:T(8,128)(2,1)} %bitcast.202), calls=%async_computation.2 | async-start | bytes 2097152 | tf_op jit(solution)/shard_map/all_to_all | solution.py:1301
  286.9 211.7 %all-gather.8.cloned.1.call-start = ((), (), s32[]{:S(2)}) async-start(), calls=%async_computation.15 | async-start | bytes 4718592 | tf_op jit(solution)/shard_map/all_gather | solution.py:1543
  336.0 39.5 %all-to-all-start.4 = ((bf16[8,1,512,128]{3,2,1,0:T(8,128)(2,1)}), bf16[8,1,512,128]{3,2,1,0:T(8,128)(2,1)}, u32[]{:S(2)}, u32[]{:S(2)}) async-start(bf16[8,1,512,128]{3,2,1,0:T(8,128)(2,1)} %bitcast.201), calls=%async_computation.4 | async-start | bytes 2097152 | tf_op jit(solution)/shard_map/all_to_all | solution.py:1301
  375.5 39.5 %all-to-all-start.5 = ((bf16[8,1,512,128]{3,2,1,0:T(8,128)(2,1)}), bf16[8,1,512,128]{3,2,1,0:T(8,128)(2,1)S(1)}, u32[]{:S(2)}, u32[]{:S(2)}) async-start(bf16[8,1,512,128]{3,2,1,0:T(8,128)(2,1)} %bitcast.198), calls=%async_computation.5 | async-start | bytes 2097152 | tf_op jit(solution)/shard_map/all_to_all | solution.py:1301
  416.0 39.6 %all-to-all-start.6 = ((bf16[8,1,512,128]{3,2,1,0:T(8,128)(2,1)}), bf16[8,1,512,128]{3,2,1,0:T(8,128)(2,1)S(1)}, u32[]{:S(2)}, u32[]{:S(2)}) async-start(bf16[8,1,512,128]{3,2,1,0:T(8,128)(2,1)} %bitcast.197), calls=%async_computation.6 | async-start | bytes 2097152 | tf_op jit(solution)/shard_map/all_to_all | solution.py:1291
  420.2 350.3 %reduce-scatter.2.cloned.1.call-start = ((), (), s32[]{:S(2)}) async-start(), calls=%async_computation.16 | async-start | bytes 19464192 | tf_op jit(solution)/shard_map/reduce_scatter | solution.py:1312
  455.6 42.9 %copy-start.14 = (bf16[8,1,512,128]{3,2,1,0:T(8,128)(2,1)}, bf16[8,1,512,128]{3,2,1,0:T(8,128)(2,1)S(1)}, u32[]{:S(2)}) copy-start(bf16[8,1,512,128]{3,2,1,0:T(8,128)(2,1)S(1)} %all-to-all-done.6) | copy-start | bytes 3145732
  501.5 74.7 %all-to-all-start.8 = ((bf16[8,1,1024,128]{3,2,1,0:T(8,128)(2,1)}), bf16[8,1,1024,128]{3,2,1,0:T(8,128)(2,1)}, u32[]{:S(2)}, u32[]{:S(2)}) async-start(bf16[8,1,1024,128]{3,2,1,0:T(8,128)(2,1)} %bitcast.53), calls=%async_computation.8 | async-start | bytes 4194304 | tf_op jit(solution)/shard_map/all_to_all | solution.py:1291
  576.2 77.5 %all-to-all-start.7 = ((bf16[8,1,512,384]{3,2,1,0:T(8,128)(2,1)}), bf16[8,1,512,384]{3,2,1,0:T(8,128)(2,1)}, u32[]{:S(2)}, u32[]{:S(2)}) async-start(bf16[8,1,512,384]{3,2,1,0:T(8,128)(2,1)} %bitcast.191), calls=%async_computation.7 | async-start | bytes 6291456 | tf_op jit(solution)/shard_map/all_to_all | solution.py:1301
  653.7 74.9 %all-to-all-start.9 = ((bf16[8,1,512,384]{3,2,1,0:T(8,128)(2,1)}), bf16[8,1,512,384]{3,2,1,0:T(8,128)(2,1)}, u32[]{:S(2)}, u32[]{:S(2)}) async-start(bf16[8,1,512,384]{3,2,1,0:T(8,128)(2,1)} %bitcast.192), calls=%async_computation.9 | async-start | bytes 6291456 | tf_op jit(solution)/shard_map/all_to_all | solution.py:1301
  728.6 41.8 %all-to-all-start.10 = ((bf16[8,1,512,384]{3,2,1,0:T(8,128)(2,1)}), bf16[8,1,512,384]{3,2,1,0:T(8,128)(2,1)}, u32[]{:S(2)}, u32[]{:S(2)}) async-start(bf16[8,1,512,384]{3,2,1,0:T(8,128)(2,1)} %bitcast.190), calls=%async_computation.10 | async-start | bytes 6291456 | tf_op jit(solution)/shard_map/all_to_all | solution.py:1301
  788.4 8.7 copy-start.29
  790.6 20.4 %collective-permute-start.1 = (bf16[4,2,2,128,768]{4,3,2,1,0:T(8,128)(2,1)S(1)}, bf16[4,2,2,128,768]{4,3,2,1,0:T(8,128)(2,1)}, u32[]{:S(2)}, u32[]{:S(2)}) collective-permute-start(bf16[4,2,2,128,768]{4,3,2,1,0:T(8,128)(2,1)S(1)} %dynamic-slice_bitcast_fusion), channel_id=1, source_target_pairs={{0,8},{8,0},{16,24},{24,16},{1,9},{9,1},{17,25},{25,17},{2,10},{10... | collective-permute-start | bytes 9437192 | tf_op jit(solution)/shard_map/ppermute | solution.py:1326
  815.0 66.4 %collective-permute-start.2 = (bf16[4,128,768]{2,1,0:T(8,128)(2,1)S(1)}, bf16[4,128,768]{2,1,0:T(8,128)(2,1)S(1)}, u32[]{:S(2)}, u32[]{:S(2)}) collective-permute-start(bf16[4,128,768]{2,1,0:T(8,128)(2,1)S(1)} %get-tuple-element.240), channel_id=1, source_target_pairs={{0,4},{8,12},{4,16},{12,24},{16,20},{24,28},{20,0},{28,8},{1,5},{9... | collective-permute-start | bytes 2359304 | tf_op jit(solution)/shard_map/ppermute | solution.py:1349
  816.3 65.1 %collective-permute-start.4 = (bf16[4,128,768]{2,1,0:T(8,128)(2,1)S(1)}, bf16[4,128,768]{2,1,0:T(8,128)(2,1)S(1)}, u32[]{:S(2)}, u32[]{:S(2)}) collective-permute-start(bf16[4,128,768]{2,1,0:T(8,128)(2,1)S(1)} %get-tuple-element.241), channel_id=1, source_target_pairs={{0,20},{8,28},{4,0},{12,8},{16,4},{24,12},{20,16},{28,24},{1,21},{... | collective-permute-start | bytes 2359304 | tf_op jit(solution)/shard_map/ppermute | solution.py:1349
  818.0 63.4 %collective-permute-start.3 = (bf16[4,128,768]{2,1,0:T(8,128)(2,1)S(1)}, bf16[4,128,768]{2,1,0:T(8,128)(2,1)S(1)}, u32[]{:S(2)}, u32[]{:S(2)}) collective-permute-start(bf16[4,128,768]{2,1,0:T(8,128)(2,1)S(1)} %get-tuple-element.242), channel_id=1, source_target_pairs={{0,16},{8,24},{4,20},{12,28},{16,0},{24,8},{20,4},{28,12},{1,17},{... | collective-permute-start | bytes 2359304 | tf_op jit(solution)/shard_map/ppermute | solution.py:1349
  820.0 60.3 %copy-start.19 = (f32[192,1024]{1,0:T(8,128)S(1)}, f32[192,1024]{1,0:T(8,128)}, u32[]{:S(2)}) copy-start(f32[192,1024]{1,0:T(8,128)} %copy-done.18) | copy-start | bytes 2359300
  880.3 10.8 %copy-start.3 = (f32[32,128]{1,0:T(8,128)}, f32[32,128]{1,0:T(8,128)S(1)}, u32[]{:S(2)}) copy-start(f32[32,128]{1,0:T(8,128)S(1)} %get-tuple-element.215) | copy-start | bytes 49156
  882.7 25.2 %all-to-all-start.11 = ((bf16[4,128,768]{2,1,0:T(8,128)(2,1)}), bf16[4,128,768]{2,1,0:T(8,128)(2,1)}, u32[]{:S(2)}, u32[]{:S(2)}) async-start(bf16[4,128,768]{2,1,0:T(8,128)(2,1)} %fusion.7), calls=%async_computation.12 | async-start | bytes 1572864 | tf_op jit(solution)/shard_map/all_to_all | solution.py:1352
  909.1 13.5 %copy-start.7 = (f32[128,768]{1,0:T(8,128)}, f32[128,768]{1,0:T(8,128)S(1)}, u32[]{:S(2)}) copy-start(f32[128,768]{1,0:T(8,128)S(1)} %convert_reduce_fusion.qkv_ref) | copy-start | bytes 1179652
  (22 other events, 68.8 us)
Sparse Core Ops, SparseCore 0:
  11.5 78.6 all-gather.3
  167.9 168.0 all-gather.5
  338.4 40.4 all-gather.7
  498.7 244.1 reduce-scatter.1
